TPU v7x, 128 devices: a whole 4x4x4 slice. The times are simulated.
128 devices in a mesh: grp: 32 (over z, x, core), tp: 4 (over y).
Axes of the slice: x: 4, y: 4, z: 4, core: 2. Of those that a mesh axis runs over, the one named last changes fastest.
Arguments:
- hidden_in: bfloat16 [1024, 2048], P('grp'), may hold values from -3 to 3
- attn_gain: float32 [2048], replicated, may hold values from 0.5 to 2
- ffn_gain: float32 [2048], replicated, may hold values from 0.5 to 2
- w_query: bfloat16 [2048, 4096], P(None, 'tp'), may hold values from -0.125 to 0.125
- w_key: bfloat16 [2048, 512], P(None, 'tp'), may hold values from -0.125 to 0.125
- w_value: bfloat16 [2048, 512], P(None, 'tp'), may hold values from -0.125 to 0.125
- q_gain: float32 [128], replicated, as said below
- k_gain: float32 [128], replicated, may hold values from 0.5 to 2
- key_cache: bfloat16 [1024, 4, 512, 128], P('grp', 'tp'), may hold values from -32 to 32
- value_cache: bfloat16 [1024, 4, 512, 128], P('grp', 'tp'), may hold values from -6 to 6
- w_out: bfloat16 [4096, 2048], P('tp'), may hold values from -0.09375 to 0.09375
- w_router: bfloat16 [2048, 128], replicated, may hold values from -0.03125 to 0.03125
- w_gate: bfloat16 [128, 2048, 768], P('grp', None, 'tp'), may hold values from -0.125 to 0.125
- w_up: bfloat16 [128, 2048, 768], P('grp', None, 'tp'), may hold values from -0.125 to 0.125
- w_down: bfloat16 [128, 768, 2048], P('grp', 'tp'), may hold values from -0.21875 to 0.21875
- cache_len: int32 [1024], P('grp'), may hold values from 1 to 512, as said below
- expert_ids: int32 [1024, 8], P('grp'), may hold values from 0 to 127, all different within a row; in each aligned block of 32 rows (0 to 31, 32 to 63, ...) at most 4 rows name the same one
Outputs:
- mixed: bfloat16 [1024, 2048], P('grp', 'tp')
Inputs may be any that keep to these rules, and one draw needn't show every extreme that they name: `expert_ids`: each row names 8 different experts. Among the 32 rows of one index of grp (aligned blocks) no expert is named by more than 4 rows, a bound that some block reaches. `cache_len`: some request has exactly 512 cached tokens. `q_gain`: positive gains.
All inputs are finite; a program needn't handle non-finite values.
Results may differ from a plain program's by a relative error of at most 0.02.
Values may be sent and summed in bfloat16 or wider, within the bound.
A program may use at most 128 MiB of HBM per device.

v0:
```python
import jax
import jax.numpy as jnp
from jax import lax
from jax.sharding import PartitionSpec as P

rope_base = 1000000.0
norm_eps = 1e-06


def rms_scale(values, gain):
    return values * lax.rsqrt(jnp.mean(values * values, axis=-1, keepdims=True) + norm_eps) * gain


def rotate(values, position):
    half_dim = values.shape[-1] // 2
    steps_half = jnp.arange(half_dim, dtype=jnp.float32)
    frequency = rope_base ** (-2.0 * steps_half / values.shape[-1])
    angle = position.astype(jnp.float32)[:, None] * frequency[None, :]
    cosine = jnp.cos(angle)[:, None, :]
    sine = jnp.sin(angle)[:, None, :]
    first = values[..., :half_dim]
    second = values[..., half_dim:]
    return jnp.concatenate(
        [first * cosine - second * sine, second * cosine + first * sine], axis=-1
    )


def attend(query, key_new, value_new, key_cache, value_cache, cache_len):
    scale = query.shape[-1] ** (-0.5)
    cached = (
        jnp.einsum("rkgd,rkpd->rkgp", query, key_cache, preferred_element_type=jnp.float32) * scale
    )
    own = jnp.einsum("rkgd,rkd->rkg", query, key_new, preferred_element_type=jnp.float32) * scale
    valid = jnp.arange(key_cache.shape[2], dtype=jnp.int32)[None, :] < cache_len[:, None]
    cached = jnp.where(valid[:, None, None, :], cached, -jnp.inf)
    highest = jnp.maximum(jnp.max(cached, axis=-1), own)
    cached_exp = jnp.exp(cached - highest[..., None])
    own_exp = jnp.exp(own - highest)
    denom = jnp.sum(cached_exp, axis=-1) + own_exp
    probs_cache = (cached_exp / denom[..., None]).astype(jnp.bfloat16)
    probs_own = (own_exp / denom).astype(jnp.bfloat16)
    result = jnp.einsum(
        "rkgp,rkpd->rkgd", probs_cache, value_cache, preferred_element_type=jnp.float32
    )
    result = (
        result
        + probs_own.astype(jnp.float32)[..., None] * value_new.astype(jnp.float32)[:, :, None, :]
    )
    return result.astype(jnp.bfloat16)


def slot_targets(ids, experts_all, capacity):
    expert_axis = jnp.arange(experts_all, dtype=jnp.int32)
    picked = jnp.sum((ids[:, :, None] == expert_axis[None, None, :]).astype(jnp.int32), axis=1)
    before = jnp.cumsum(picked, axis=0) - picked
    slot = jnp.take_along_axis(before, ids, axis=1)
    return ids * capacity + slot


def place_rows(targets, values, slot_count):
    slot_axis = jnp.arange(slot_count, dtype=jnp.int32)
    placing = jnp.any(slot_axis[:, None, None] == targets[None, :, :], axis=2).astype(values.dtype)
    return jnp.dot(placing, values, preferred_element_type=jnp.float32).astype(jnp.bfloat16)


def combine_rows(targets, weights, returned):
    slot_axis = jnp.arange(returned.shape[0], dtype=jnp.int32)
    mixing = jnp.sum(
        jnp.where(targets[:, :, None] == slot_axis[None, None, :], weights[:, :, None], 0.0), axis=1
    )
    return jnp.dot(mixing, returned.astype(jnp.float32), precision=lax.Precision.HIGHEST)


def per_device(
    hidden_in,
    attn_gain,
    ffn_gain,
    w_query,
    w_key,
    w_value,
    q_gain,
    k_gain,
    key_cache,
    value_cache,
    w_out,
    w_router,
    w_gate,
    w_up,
    w_down,
    cache_len,
    expert_ids,
):
    tok_rows = hidden_in.shape[0]
    width = hidden_in.shape[1]
    head_dim = q_gain.shape[0]
    kv_local = key_cache.shape[1]
    experts_all = w_router.shape[1]
    top_count = expert_ids.shape[1]
    capacity = max(2, 2 * tok_rows * top_count // experts_all)
    quarter = width // lax.axis_size("tp")
    tp_index = lax.axis_index("tp")
    residual_in = hidden_in.astype(jnp.float32)
    normed = rms_scale(residual_in, attn_gain).astype(jnp.bfloat16)
    query = jnp.dot(normed, w_query, preferred_element_type=jnp.float32).reshape(
        tok_rows, -1, head_dim
    )
    key_new = jnp.dot(normed, w_key, preferred_element_type=jnp.float32).reshape(
        tok_rows, kv_local, head_dim
    )
    value_new = (
        jnp.dot(normed, w_value, preferred_element_type=jnp.float32)
        .reshape(tok_rows, kv_local, head_dim)
        .astype(jnp.bfloat16)
    )
    query = (
        rotate(rms_scale(query, q_gain), cache_len)
        .astype(jnp.bfloat16)
        .reshape(tok_rows, kv_local, -1, head_dim)
    )
    key_new = rotate(rms_scale(key_new, k_gain), cache_len).astype(jnp.bfloat16)
    attended = attend(query, key_new, value_new, key_cache, value_cache, cache_len).reshape(
        tok_rows, -1
    )
    head_terms = jnp.dot(attended, w_out, preferred_element_type=jnp.float32)
    mid = residual_in + lax.psum(head_terms.astype(jnp.bfloat16), "tp").astype(jnp.float32)
    ffn_in = rms_scale(mid, ffn_gain).astype(jnp.bfloat16)
    logits = jnp.dot(ffn_in, w_router, preferred_element_type=jnp.float32)
    weights = jax.nn.softmax(jnp.take_along_axis(logits, expert_ids, axis=1), axis=-1)
    targets = slot_targets(expert_ids, experts_all, capacity)
    sent = place_rows(targets, ffn_in, experts_all * capacity).reshape(experts_all, capacity, width)
    received = lax.all_to_all(sent, "grp", split_axis=0, concat_axis=1, tiled=True)
    gate = jnp.einsum("esd,edf->esf", received, w_gate, preferred_element_type=jnp.float32)
    upper = jnp.einsum("esd,edf->esf", received, w_up, preferred_element_type=jnp.float32)
    active = (jax.nn.silu(gate) * upper).astype(jnp.bfloat16)
    expert_terms = jnp.einsum("esf,efd->esd", active, w_down, preferred_element_type=jnp.float32)
    summed = lax.psum(expert_terms.astype(jnp.bfloat16), "tp")
    back_full = lax.all_to_all(summed, "grp", split_axis=1, concat_axis=0, tiled=True)
    returned = lax.dynamic_slice_in_dim(back_full, tp_index * quarter, quarter, 2)
    own_mid = lax.dynamic_slice_in_dim(mid, tp_index * quarter, quarter, 1)
    expert_mix = combine_rows(targets, weights, returned.reshape(experts_all * capacity, quarter))
    return (own_mid + expert_mix).astype(jnp.bfloat16)


def solution(mesh):
    in_specs = (
        P("grp", None),
        P(),
        P(),
        P(None, "tp"),
        P(None, "tp"),
        P(None, "tp"),
        P(),
        P(),
        P("grp", "tp", None, None),
        P("grp", "tp", None, None),
        P("tp", None),
        P(),
        P("grp", None, "tp"),
        P("grp", None, "tp"),
        P("grp", "tp", None),
        P("grp"),
        P("grp", None),
    )
    out_specs = P("grp", "tp")
    return jax.shard_map(
        per_device, mesh=mesh, in_specs=in_specs, out_specs=out_specs, check_vma=False
    )
```

profile of v0, /device:TPU:0, one launch (start us, length us, event | category | flops | bytes accessed | tf_op | source)
XLA Modules:
  0.0 237.2 jit_solution(8427285358094215140)
XLA Ops:
  8.3 1.0 fusion.26
  9.3 3.3 %convolution_bitcast_fusion = f32[4,8,8,128]{3,1,2,0:T(8,128)S(1)} fusion(bf16[2048,1024]{1,0:T(8,128)(2,1)} %param.20, bf16[32,2048]{1,0:T(8,128)(2,1)} %param.17, f32[2048]{0:T(1024)} %param.18, f32[32]{0:T(128)S(1)} %add_rsqrt_fusion.3), kind=kOutput, calls=%fused_computation.15 | convolution fusion | flops 134479872 | bytes 4464768 | tf_op jit(solution)/shard_map/dot_general | solution.py:104
  14.2 1.3 fusion.59
  17.9 1.5 convolution_convert_fusion.2
  19.8 1.9 gather_fusion
  22.1 41.1 %all-reduce.3.cloned.1.call-done = bf16[32,2048]{1,0:T(8,128)(2,1)} async-done(((bf16[32,2048]{1,0:T(8,128)(2,1)}), bf16[32,2048]{1,0:T(8,128)(2,1)}) %all-reduce.3.cloned.1.call-update) | async-done | bytes 131088 | tf_op jit(solution)/shard_map/psum | solution.py:125
  63.2 1.8 convert_add_fusion
  65.0 3.0 %convolution_convert_fusion.1 = bf16[512,2048]{1,0:T(8,128)(2,1)} fusion(pred[512,32]{0,1:T(8,128)(4,1)S(1)} %fusion.19, f32[2048]{0:T(1024)S(1)} %copy-done.9, f32[32]{0:T(128)S(1)} %add_rsqrt_fusion.1, bf16[32,2048]{1,0:T(8,128)(2,1)} %all-reduce.3.cloned.1.call-done, bf16[32,2048]{1,0:T(8,128)(2,1)S(1)} %copy-done.1), kind=kOutput, calls=%fused_computation.7 | convolution fusion | flops 68550656 | bytes 2384000 | tf_op jit(solution)/shard_map/dot_general | solution.py:63
  68.0 4.1 %reshape.294 = bf16[128,4,2048]{2,1,0:T(4,128)(2,1)} reshape(bf16[512,2048]{1,0:T(8,128)(2,1)} %convolution_convert_fusion.1) | data formatting | bytes 4194304 | tf_op jit(solution)/shard_map/reshape | solution.py:130
  72.1 35.8 %all_to_all.36 = bf16[128,4,2048]{2,1,0:T(4,128)(2,1)S(1)} all-to-all(bf16[128,4,2048]{2,1,0:T(4,128)(2,1)} %reshape.294), channel_id=1, replica_groups=mesh['grp'=32,'tp'=4] {'grp'}, dimensions={0} | all-to-all | bytes 4194304 | tf_op jit(solution)/shard_map/all_to_all | solution.py:131
  107.9 2.6 %copy.57 = bf16[32,4,4,2048]{3,2,0,1:T(4,128)(2,1)} copy(bf16[32,4,4,2048]{3,2,1,0:T(4,128)(2,1)S(1)} %bitcast.59) | data formatting | bytes 4194304 | tf_op jit(solution)/shard_map/all_to_all | solution.py:131
  110.5 4.0 %all_to_all.29 = bf16[4,128,2048]{2,1,0:T(8,128)(2,1)} reshape(bf16[4,32,4,2048]{3,2,1,0:T(4,128)(2,1)} %bitcast.60) | data formatting | bytes 4194304 | tf_op jit(solution)/shard_map/all_to_all | solution.py:131
  114.5 4.2 %fusion.60 = f32[4,128,192]{1,2,0:T(8,128)} fusion(bf16[4,128,2048]{2,1,0:T(8,128)(2,1)} %all_to_all.29, bf16[4,2048,192]{1,2,0:T(8,128)(2,1)} %param.29), kind=kOutput, calls=%fused_computation.99 | convolution fusion | flops 402653184 | bytes 5636096 | tf_op jit(solution)/shard_map/esd,edf->esf/dot_general | solution.py:132
  118.7 5.4 %convolution_convert_fusion = bf16[4,128,2048]{2,1,0:T(8,128)(2,1)} fusion(bf16[4,192,2048]{2,1,0:T(8,128)(2,1)S(1)} %copy-done, bf16[4,128,2048]{2,1,0:T(8,128)(2,1)} %all_to_all.29, bf16[4,2048,192]{1,2,0:T(8,128)(2,1)} %param.30, f32[4,128,192]{1,2,0:T(8,128)} %fusion.60), kind=kOutput, calls=%fused_computation.6 | convolution fusion | flops 806944768 | bytes 10878976 | tf_op jit(solution)/shard_map/esf,efd->esd/dot_general | solution.py:135
  124.1 55.6 %all-reduce.5.cloned.1.call-done = bf16[4,128,2048]{2,1,0:T(8,128)(2,1)} async-done(((bf16[4,128,2048]{2,1,0:T(8,128)(2,1)}), bf16[4,128,2048]{2,1,0:T(8,128)(2,1)}) %all-reduce.5.cloned.1.call-update) | async-done | bytes 2097168 | tf_op jit(solution)/shard_map/psum | solution.py:136
  179.7 4.6 %copy.44 = bf16[4,128,2048]{2,0,1:T(4,128)(2,1)} copy(bf16[4,128,2048]{2,1,0:T(8,128)(2,1)} %all-reduce.5.cloned.1.call-done) | data formatting | bytes 4194304 | tf_op jit(solution)/shard_map/psum | solution.py:136
  184.3 7.7 %all-to-all-start.1 = ((bf16[4,128,2048]{2,0,1:T(4,128)(2,1)}), bf16[4,128,2048]{2,0,1:T(4,128)(2,1)}, u32[]{:S(2)}, u32[]{:S(2)}) async-start(bf16[4,128,2048]{2,0,1:T(4,128)(2,1)} %copy.44), calls=%async_computation.1 | async-start | bytes 4194304 | tf_op jit(solution)/shard_map/all_to_all | solution.py:137
  192.0 1.3 fusion.54
  193.3 1.9 gather_fusion.1
  195.9 25.8 %all-to-all-done.1 = bf16[4,128,2048]{2,0,1:T(4,128)(2,1)} async-done(((bf16[4,128,2048]{2,0,1:T(4,128)(2,1)}), bf16[4,128,2048]{2,0,1:T(4,128)(2,1)}, u32[]{:S(2)}, u32[]{:S(2)}) %all-to-all-start.1) | async-done | bytes 2097184 | tf_op jit(solution)/shard_map/all_to_all | solution.py:137
  221.8 3.6 %copy.45 = bf16[4,32,4,2048]{3,2,0,1:T(4,128)(2,1)S(1)} copy(bf16[4,32,4,2048]{3,0,2,1:T(4,128)(2,1)} %bitcast.11) | data formatting | bytes 4194304 | tf_op jit(solution)/shard_map/all_to_all | solution.py:137
  225.3 1.1 constant_dynamic-slice_fusion
  226.4 2.0 reshape.295
  228.3 2.0 fusion.17
  (66 shorter events, 7.0 us)
Async XLA Ops:
  6.5 112.2 %copy-start = (bf16[4,192,2048]{2,1,0:T(8,128)(2,1)S(1)}, bf16[4,192,2048]{2,1,0:T(8,128)(2,1)}, u32[]{:S(2)}) copy-start(bf16[4,192,2048]{2,1,0:T(8,128)(2,1)} %param.31) | copy-start | bytes 9437188
  6.5 6.3 %copy-start.1 = (bf16[32,2048]{1,0:T(8,128)(2,1)S(1)}, bf16[32,2048]{1,0:T(8,128)(2,1)}, u32[]{:S(2)}) copy-start(bf16[32,2048]{1,0:T(8,128)(2,1)} %param.17) | copy-start | bytes 393220
  6.5 6.3 %copy-start.8 = (f32[2048]{0:T(1024)S(1)}, f32[2048]{0:T(1024)}, u32[]{:S(2)}) copy-start(f32[2048]{0:T(1024)} %param.18) | copy-start | bytes 24580
  6.5 6.8 %copy-start.11 = (f32[128]{0:T(128)S(1)}, f32[128]{0:T(128)}, u32[]{:S(2)}) copy-start(f32[128]{0:T(128)} %param.24) | copy-start | bytes 1540
  6.5 7.0 %copy-start.12 = (f32[128]{0:T(128)S(1)}, f32[128]{0:T(128)}, u32[]{:S(2)}) copy-start(f32[128]{0:T(128)} %param.23) | copy-start | bytes 1540
  6.5 56.6 %all-reduce.3.cloned.1.call-start = ((), (), s32[]{:S(2)}) async-start(), calls=%async_computation.2 | async-start | bytes 262144 | tf_op jit(solution)/shard_map/psum | solution.py:125
  6.6 6.2 %copy-start.6 = (bf16[2048,128]{1,0:T(8,128)(2,1)S(1)}, bf16[2048,128]{1,0:T(8,128)(2,1)}, u32[]{:S(2)}) copy-start(bf16[2048,128]{1,0:T(8,128)(2,1)} %param.21) | copy-start | bytes 1572868
  9.3 4.8 %copy-start.2 = (bf16[32,1,512,128]{3,2,1,0:T(8,128)(2,1)S(1)}, bf16[32,1,512,128]{3,2,1,0:T(8,128)(2,1)}, u32[]{:S(2)}) copy-start(bf16[32,1,512,128]{3,2,1,0:T(8,128)(2,1)} %param.25) | copy-start | bytes 12582916
  13.7 2.0 copy-start.7
  14.1 2.2 copy-start.3
  15.5 2.4 %copy-start.4 = (bf16[1024,2048]{1,0:T(8,128)(2,1)S(1)}, bf16[1024,2048]{1,0:T(8,128)(2,1)}, u32[]{:S(2)}) copy-start(bf16[1024,2048]{1,0:T(8,128)(2,1)} %param.27) | copy-start | bytes 12582916
  17.1 2.3 copy-start.10
  19.4 160.4 %all-reduce.5.cloned.1.call-start = ((), (), s32[]{:S(2)}) async-start(), calls=%async_computation.3 | async-start | bytes 4194304 | tf_op jit(solution)/shard_map/psum | solution.py:136
  19.8 45.1 %copy-start.9 = (f32[2048]{0:T(1024)S(1)}, f32[2048]{0:T(1024)}, u32[]{:S(2)}) copy-start(f32[2048]{0:T(1024)} %param.19) | copy-start | bytes 24580
  184.3 7.7 %copy-start.5 = (bf16[32,2048]{1,0:T(8,128)(2,1)S(1)}, bf16[32,2048]{1,0:T(8,128)(2,1)}, u32[]{:S(2)}) copy-start(bf16[32,2048]{1,0:T(8,128)(2,1)} %all-reduce.3.cloned.1.call-done) | copy-start | bytes 393220
  184.3 37.5 %all-to-all-start.1 = ((bf16[4,128,2048]{2,0,1:T(4,128)(2,1)}), bf16[4,128,2048]{2,0,1:T(4,128)(2,1)}, u32[]{:S(2)}, u32[]{:S(2)}) async-start(bf16[4,128,2048]{2,0,1:T(4,128)(2,1)} %copy.44), calls=%async_computation.1 | async-start | bytes 4194304 | tf_op jit(solution)/shard_map/all_to_all | solution.py:137
Sparse Core Ops, SparseCore 0:
  19.5 43.6 all-reduce.2
  124.2 55.4 all-reduce.4
where the time goes:
time: 238 us; the launch traced here: 237 us
  waiting for transfers between devices  123 us (52%)
  blocking collectives  35.8 us (15%)
  local copies, waits for them, and re-layouts  27.2 us (11%)
  matrix products  23.6 us (10%)
  between operations  13.7 us (6%)
  starting transfers between devices  7.75 us (3%)
  other arithmetic  6.54 us (3%)
    psum x1, waiting for transfers between devices, per_device(): summed = lax.psum(expert_terms.astype(jnp.bfloat16), 'tp')  55.6 us
    psum x1, waiting for transfers between devices, per_device(): lax.psum(head_terms.astype(jnp.bfloat16), 'tp').astype(jnp.float32)  41.1 us
    all_to_all x1, blocking collectives, per_device(): lax.all_to_all(sent, 'grp', split_axis=0, concat_axis=1, tiled=True)  35.8 us
    all_to_all x1, waiting for transfers between devices, per_device(): lax.all_to_all(summed, 'grp', split_axis=1, concat_axis=0, tiled=True)  25.8 us
    all_to_all x1, starting transfers between devices, per_device(): lax.all_to_all(summed, 'grp', split_axis=1, concat_axis=0, tiled=True)  7.67 us
    all_to_all x2, local copies, waits for them, and re-layouts, per_device(): lax.all_to_all(sent, 'grp', split_axis=0, concat_axis=1, tiled=True)  6.55 us
    dot_general x1, matrix products, per_device(): jnp.einsum('esf,efd->esd', active, w_down, preferred_element_type=jnp.flo...  5.38 us
  transfers between devices with their start and end apart: 3, of which 3 were waited for; matrix products, arithmetic and copies ran while one was open for 3% of the time, Pallas kernels for 0%

commit v1 on v0

v1 whole, which is shorter than its diff:
```python
import jax
import jax.numpy as jnp
from jax import lax
from jax.experimental import pallas as pl
from jax.experimental.pallas import tpu as pltpu
from jax.sharding import PartitionSpec as P

rope_base = 1000000.0
norm_eps = 1e-06
MESH = pl.DeviceIdType.MESH
BF = jnp.bfloat16
F32 = jnp.float32

ORDER_A = ("x", "y", "z")
ORDER_B = ("y", "z", "x")
ORDER_C = ("z", "x", "y")


def rms_scale(values, gain):
    return values * lax.rsqrt(jnp.mean(values * values, axis=-1, keepdims=True) + norm_eps) * gain


def rotate(values, position):
    half_dim = values.shape[-1] // 2
    steps_half = jnp.arange(half_dim, dtype=jnp.float32)
    frequency = rope_base ** (-2.0 * steps_half / values.shape[-1])
    angle = position.astype(jnp.float32)[:, None] * frequency[None, :]
    cosine = jnp.cos(angle)[:, None, :]
    sine = jnp.sin(angle)[:, None, :]
    first = values[..., :half_dim]
    second = values[..., half_dim:]
    return jnp.concatenate(
        [first * cosine - second * sine, second * cosine + first * sine], axis=-1
    )


def attend(query, key_new, value_new, key_cache, value_cache, cache_len):
    scale = query.shape[-1] ** (-0.5)
    cached = (
        jnp.einsum("rkgd,rkpd->rkgp", query, key_cache, preferred_element_type=jnp.float32) * scale
    )
    own = jnp.einsum("rkgd,rkd->rkg", query, key_new, preferred_element_type=jnp.float32) * scale
    valid = jnp.arange(key_cache.shape[2], dtype=jnp.int32)[None, :] < cache_len[:, None]
    cached = jnp.where(valid[:, None, None, :], cached, -jnp.inf)
    highest = jnp.maximum(jnp.max(cached, axis=-1), own)
    cached_exp = jnp.exp(cached - highest[..., None])
    own_exp = jnp.exp(own - highest)
    denom = jnp.sum(cached_exp, axis=-1) + own_exp
    probs_cache = (cached_exp / denom[..., None]).astype(jnp.bfloat16)
    probs_own = (own_exp / denom).astype(jnp.bfloat16)
    result = jnp.einsum(
        "rkgp,rkpd->rkgd", probs_cache, value_cache, preferred_element_type=jnp.float32
    )
    result = (
        result
        + probs_own.astype(jnp.float32)[..., None] * value_new.astype(jnp.float32)[:, :, None, :]
    )
    return result.astype(jnp.bfloat16)


def dot(a, b):
    return jnp.dot(a, b, preferred_element_type=F32)


def coords():
    g = lax.axis_index("grp")
    return {"z": g // 8, "x": (g // 2) % 4, "c": g % 2, "y": lax.axis_index("tp")}


def device(co):
    return ((co["z"] * 4 + co["x"]) * 2 + co["c"], co["y"])


def moved(co, axis, d):
    size = 2 if axis == "c" else 4
    return dict(co, **{axis: (co[axis] + d) % size})


def block(ref, q, free, co):
    at = [slice(None) if a in free else co[a] for a in ("y", "z", "x")]
    return ref.at[q, at[0], at[1], at[2], co["c"]]


def moe_kernel(
    terms, hidden, gain, ids, w_router, wg_hbm, wu_hbm, wd_hbm,
    out_ref,
    wg, wu, wd, tin, ids_all, xa, xs, sel, msel, wslot, oslot, ya, ysib, r1, s1, r2, s2, r3, mid_ref,
    wsem, t_send, t_recv, i_send, i_recv, g_send, g_recv, c_send, c_recv, e_send, e_recv, s_send, s_recv,
):
    co = coords()
    grp = lax.axis_index("grp")
    me_y = co["y"]
    me_c = co["c"]
    sibling = moved(co, "c", 1)

    def remote(src, dst, ss, rs, to):
        return pltpu.make_async_remote_copy(
            src_ref=src, dst_ref=dst, send_sem=ss, recv_sem=rs, device_id=device(to),
            device_id_type=MESH,
        )

    loads = [
        pltpu.make_async_copy(s, d, wsem.at[i])
        for i, (s, d) in enumerate(((wg_hbm, wg), (wu_hbm, wu), (wd_hbm, wd)))
    ]
    for cp in loads:
        cp.start()

    bar = pltpu.get_barrier_semaphore()

    def greet(d, _):
        pl.semaphore_signal(bar, inc=1, device_id=((grp + d) % 32, me_y), device_id_type=MESH)
        return 0

    lax.fori_loop(1, 32, greet, 0)
    for d in (1, 2, 3):
        pl.semaphore_signal(bar, inc=1, device_id=device(moved(co, "y", d)), device_id_type=MESH)
    lane = lax.broadcasted_iota(jnp.int32, (8, 128), 1)
    idv = ids[...]
    ids_all[grp] = jnp.where(lane // 32 == grp % 4, jnp.concatenate([idv] * 4, axis=1), -1)
    pl.semaphore_wait(bar, 34)

    def quarter(v):
        return pl.ds(pl.multiple_of(v * 512, 512), 512)

    t_copies = []
    for d in (1, 2, 3):
        to = moved(co, "y", d)
        cp = remote(terms.at[:, quarter(to["y"])], tin.at[d - 1], t_send.at[d - 1], t_recv.at[d - 1], to)
        cp.start()
        t_copies.append(cp)

    def ids_copy(d):
        return pltpu.make_async_remote_copy(
            src_ref=ids_all.at[grp], dst_ref=ids_all.at[grp], send_sem=i_send.at[d],
            recv_sem=i_recv.at[d], device_id=((grp + d) % 32, me_y), device_id_type=MESH,
        )

    def ids_start(d, _):
        ids_copy(d).start()
        return 0

    lax.fori_loop(1, 32, ids_start, 0)
    mid = hidden[:, quarter(me_y)].astype(F32) + terms[:, quarter(me_y)].astype(F32)
    for d in (1, 2, 3):
        t_copies[d - 1].wait_recv()
        mid = mid + tin[d - 1].astype(F32)
    mid_ref[...] = mid
    sent = (mid * gain[:, quarter(me_y)]).astype(BF)
    for q in range(4):
        xa[q, me_y, co["z"], co["x"], me_c] = sent[:, q * 128 : (q + 1) * 128]

    def ag_copy(q, order, k, d):
        part = block(xa, q, order[:k], co)
        return remote(part, part, g_send.at[q, k, d - 1], g_recv.at[q, k, d - 1], moved(co, order[k], d))

    def sib_copy(q, order, j):
        part = block(xa, q, order[:2], moved(co, order[2], -j))
        return remote(part, part, c_send.at[q, j], c_recv.at[q, j], sibling)

    def each_part(fn):
        fn(0, ORDER_A)
        fn(1, ORDER_B)
        fn(2, ORDER_C)
        pl.when(me_c == 0)(lambda: fn(3, ORDER_A))
        pl.when(me_c == 1)(lambda: fn(3, ORDER_B))

    def ag_start(k):
        def go(q, order):
            if k > 0:
                for d in (1, 2, 3):
                    ag_copy(q, order, k - 1, d).wait_recv()
            for d in (1, 2, 3):
                ag_copy(q, order, k, d).start()
            if k == 2:
                sib_copy(q, order, 0).start()

        each_part(go)

    ag_start(0)

    def ids_wait(d, _):
        ids_copy(d).wait_recv()
        return 0

    lax.fori_loop(1, 32, ids_wait, 0)
    row = lax.broadcasted_iota(jnp.int32, (256, 256), 0)
    col = lax.broadcasted_iota(jnp.int32, (256, 256), 1)
    before = jnp.where((row < col) & (row // 32 == col // 32), 1.0, 0.0).astype(BF)
    lane256 = lax.broadcasted_iota(jnp.int32, (8, 256), 1)
    sub8 = lax.broadcasted_iota(jnp.int32, (8, 256), 0)
    sub32 = lax.broadcasted_iota(jnp.int32, (32, 256), 0)
    sub128 = lax.broadcasted_iota(jnp.int32, (128, 256), 0)

    def make_slots(z):
        halves = []
        for h in (0, 1):
            t = ids_all[z * 8 + h * 4]
            for j in (1, 2, 3):
                t = jnp.maximum(t, ids_all[z * 8 + h * 4 + j])
            halves.append(t)
        idz = jnp.concatenate(halves, axis=1)
        picked = jnp.zeros((8, 256), F32)
        chosen = jnp.zeros((128, 256), F32)
        for k in range(8):
            row_k = idz[k : k + 1, :]
            picked = picked + jnp.where(row_k == grp * 4 + sub8, 1.0, 0.0)
            chosen = chosen + jnp.where(row_k == sub128, 1.0, 0.0)
        rank = dot(picked.astype(BF), before).astype(jnp.int32)
        place = jnp.where(picked > 0.5, (lane256 // 32) * 4 + rank, -1)
        for e in range(4):
            sel[z, e * 32 : (e + 1) * 32, :] = jnp.where(sub32 == place[e : e + 1, :], 1.0, 0.0).astype(BF)
        ms = lax.dot_general(
            sel[z], chosen.astype(BF), (((1,), (1,)), ((), ())), preferred_element_type=F32
        )
        for e in range(4):
            msel[e, z * 32 : (z + 1) * 32, :] = ms[e * 32 : (e + 1) * 32]

    ag_start(1)
    make_slots(0)
    make_slots(1)
    ag_start(2)
    make_slots(2)
    make_slots(3)

    def ag_last(q, order):
        for d in (1, 2, 3):
            ag_copy(q, order, 2, d).wait_recv()
            sib_copy(q, order, d).start()

    each_part(ag_last)

    def ag_sib(q, order):
        for j in range(4):
            sib_copy(q, order, j).wait_recv()

    def select(q):
        for z in range(4):
            for y in range(4):
                rows = dot(sel[z], xa[q, y, z].reshape(256, 128)).astype(BF)
                for e in range(4):
                    xs[e, z * 32 : (z + 1) * 32, y * 512 + q * 128 : y * 512 + (q + 1) * 128] = rows[
                        e * 32 : (e + 1) * 32
                    ]

    ag_sib(0, ORDER_A)
    select(0)
    ag_sib(1, ORDER_B)
    select(1)
    ag_sib(2, ORDER_C)
    select(2)
    pl.when(me_c == 0)(lambda: ag_sib(3, ORDER_A))
    pl.when(me_c == 1)(lambda: ag_sib(3, ORDER_B))
    select(3)

    for cp in loads:
        cp.wait()
    inv_gain = 1.0 / gain[...]
    lane128 = lax.broadcasted_iota(jnp.int32, (128, 128), 1)
    for e in range(4):
        rows = xs[e]
        plain = rows.astype(F32) * inv_gain
        scale = lax.rsqrt(jnp.sum(plain * plain, axis=1, keepdims=True) * (1.0 / 2048) + norm_eps)
        logits = dot(rows, w_router[...]) * scale
        on = msel[e] > 0.5
        top = jnp.max(jnp.where(on, logits, -1e30), axis=1, keepdims=True)
        ex = jnp.where(on, jnp.exp(jnp.where(on, logits - top, 0.0)), 0.0)
        total = jnp.sum(ex, axis=1, keepdims=True)
        mine = jnp.sum(jnp.where(lane128 == grp * 4 + e, ex, 0.0), axis=1, keepdims=True)
        weight = mine / jnp.where(total > 0.0, total, 1.0)
        gate = dot(rows, wg[e]) * scale
        upper = dot(rows, wu[e]) * scale
        active = (gate / (1.0 + jnp.exp(-gate)) * upper).astype(BF)
        res = (dot(active, wd[e]) * weight).astype(BF)
        for z in range(4):
            oslot[z, e * 32 : (e + 1) * 32, :] = res[z * 32 : (z + 1) * 32]

    def pair_copy(z):
        return remote(
            ya.at[:, :, z, :, 1 - me_c], ysib.at[:, :, z], e_send.at[z], e_recv.at[z], sibling
        )

    for z in range(4):
        for y in range(4):
            part = lax.dot_general(
                sel[z], oslot[z, :, y * 512 : (y + 1) * 512], (((0,), (0,)), ((), ())),
                preferred_element_type=F32,
            ).astype(BF)
            for q in range(4):
                ya[q, y, z] = part[:, q * 128 : (q + 1) * 128].reshape(4, 2, 32, 128)
        pair_copy(z).start()
    for z in range(4):
        pair_copy(z).wait()
        for q in range(4):
            mine = ya.at[q, :, z, :, me_c]
            mine[...] = (mine[...].astype(F32) + ysib[q, :, z].astype(F32)).astype(BF)

    def rs_copy(q, order, k, d):
        axis = order[2 - k]
        to = moved(co, axis, d)
        if k == 0:
            src = block(ya, q, [a for a in order if a != axis], to)
            dst = r1.at[q, d - 1]
        elif k == 1:
            left = [a for a in ("y", "z", "x") if a != order[2]]
            src = s1.at[q, to[axis]] if left[0] == axis else s1.at[q, :, to[axis]]
            dst = r2.at[q, d - 1]
        else:
            src = s2.at[q, to[axis]]
            dst = r3.at[q, d - 1]
        return remote(src, dst, s_send.at[q, k, d - 1], s_recv.at[q, k, d - 1], to)

    def rs_start(k):
        def go(q, order):
            for d in (1, 2, 3):
                rs_copy(q, order, k, d).start()

        return go

    def rs_sum(k):
        def go(q, order):
            for d in (1, 2, 3):
                rs_copy(q, order, k, d).wait_recv()
            if k == 0:
                own = block(ya, q, order[:2], co)[...].astype(F32)
                s1[q] = (own + r1[q, 0].astype(F32) + r1[q, 1].astype(F32) + r1[q, 2].astype(F32)).astype(BF)
            elif k == 1:
                axis = order[1]
                left = [a for a in ("y", "z", "x") if a != order[2]]
                own = s1[q, co[axis]] if left[0] == axis else s1[q, :, co[axis]]
                own = own.astype(F32)
                s2[q] = (own + r2[q, 0].astype(F32) + r2[q, 1].astype(F32) + r2[q, 2].astype(F32)).astype(BF)
            else:
                own = s2[q, co[order[0]]].astype(F32)
                cols = slice(q * 128, (q + 1) * 128)
                out_ref[:, cols] = (
                    mid_ref[:, cols]
                    + ((own + r3[q, 0].astype(F32)) + (r3[q, 1].astype(F32) + r3[q, 2].astype(F32)))
                ).astype(BF)

        return go

    each_part(rs_start(0))
    for k in (0, 1):

        def step(q, order, k=k):
            rs_sum(k)(q, order)
            rs_start(k + 1)(q, order)

        each_part(step)
    each_part(rs_sum(2))

    for cp in t_copies:
        cp.wait_send()

    def ids_sent(d, _):
        ids_copy(d).wait_send()
        return 0

    lax.fori_loop(1, 32, ids_sent, 0)

    def sent_all(q, order):
        for k in range(3):
            for d in (1, 2, 3):
                ag_copy(q, order, k, d).wait_send()
                rs_copy(q, order, k, d).wait_send()
        for j in range(4):
            sib_copy(q, order, j).wait_send()

    each_part(sent_all)


def moe(terms, hidden, gain, ids, w_router, w_gate, w_up, w_down):
    vm = pl.BlockSpec(memory_space=pltpu.VMEM)
    hbm = pl.BlockSpec(memory_space=pl.ANY)
    dma = pltpu.SemaphoreType.DMA
    return pl.pallas_call(
        moe_kernel,
        out_shape=jax.ShapeDtypeStruct((32, 512), BF),
        in_specs=[vm] * 5 + [hbm] * 3,
        out_specs=vm,
        scratch_shapes=[
            pltpu.VMEM((4, 2048, 192), BF),
            pltpu.VMEM((4, 2048, 192), BF),
            pltpu.VMEM((4, 192, 2048), BF),
            pltpu.VMEM((3, 32, 512), BF),
            pltpu.VMEM((32, 8, 128), jnp.int32),
            pltpu.VMEM((4, 4, 4, 4, 2, 32, 128), BF),
            pltpu.VMEM((4, 128, 2048), BF),
            pltpu.VMEM((4, 128, 256), BF),
            pltpu.VMEM((4, 128, 128), F32),
            pltpu.VMEM((4, 128, 128), F32),
            pltpu.VMEM((4, 128, 2048), BF),
            pltpu.VMEM((4, 4, 4, 4, 2, 32, 128), BF),
            pltpu.VMEM((4, 4, 4, 4, 32, 128), BF),
            pltpu.VMEM((4, 3, 4, 4, 32, 128), BF),
            pltpu.VMEM((4, 4, 4, 32, 128), BF),
            pltpu.VMEM((4, 3, 4, 32, 128), BF),
            pltpu.VMEM((4, 4, 32, 128), BF),
            pltpu.VMEM((4, 3, 32, 128), BF),
            pltpu.VMEM((32, 512), F32),
            dma((3,)), dma((3,)), dma((3,)), dma((32,)), dma((32,)),
            dma((4, 3, 3)), dma((4, 3, 3)), dma((4, 4)), dma((4, 4)), dma((4,)), dma((4,)),
            dma((4, 3, 3)), dma((4, 3, 3)),
        ],
        compiler_params=pltpu.CompilerParams(
            collective_id=0, has_side_effects=True, vmem_limit_bytes=56 << 20
        ),
        name="moe",
    )(terms, hidden, gain, ids, w_router, w_gate, w_up, w_down)


def per_device(
    hidden_in, attn_gain, ffn_gain, w_query, w_key, w_value, q_gain, k_gain, key_cache,
    value_cache, w_out, w_router, w_gate, w_up, w_down, cache_len, expert_ids,
):
    tok_rows = hidden_in.shape[0]
    head_dim = q_gain.shape[0]
    kv_local = key_cache.shape[1]
    residual_in = hidden_in.astype(jnp.float32)
    normed = rms_scale(residual_in, attn_gain).astype(jnp.bfloat16)
    query = dot(normed, w_query).reshape(tok_rows, -1, head_dim)
    key_new = dot(normed, w_key).reshape(tok_rows, kv_local, head_dim)
    value_new = dot(normed, w_value).reshape(tok_rows, kv_local, head_dim).astype(jnp.bfloat16)
    query = (
        rotate(rms_scale(query, q_gain), cache_len)
        .astype(jnp.bfloat16)
        .reshape(tok_rows, kv_local, -1, head_dim)
    )
    key_new = rotate(rms_scale(key_new, k_gain), cache_len).astype(jnp.bfloat16)
    attended = attend(query, key_new, value_new, key_cache, value_cache, cache_len).reshape(
        tok_rows, -1
    )
    terms = dot(attended, w_out).astype(BF)
    return moe(
        terms, hidden_in, ffn_gain.reshape(1, -1), expert_ids.T, w_router, w_gate, w_up, w_down
    )


def solution(mesh):
    in_specs = (
        P("grp", None), P(), P(), P(None, "tp"), P(None, "tp"), P(None, "tp"), P(), P(),
        P("grp", "tp", None, None), P("grp", "tp", None, None), P("tp", None), P(),
        P("grp", None, "tp"), P("grp", None, "tp"), P("grp", "tp", None), P("grp"), P("grp", None),
    )
    return jax.shard_map(
        per_device, mesh=mesh, in_specs=in_specs, out_specs=P("grp", "tp"), check_vma=False
    )
```

time: 238 us -> 92.3 us (0.39)
  waiting for transfers between devices: 123 us -> 0 us
  Pallas kernels: 0 us -> 63.3 us
  blocking collectives: 35.8 us -> 0 us
  matrix products: 23.6 us -> 9.54 us
  between operations: 13.7 us -> 0.15 us
  local copies, waits for them, and re-layouts: 27.2 us -> 14.1 us
  starting transfers between devices: 7.75 us -> 0 us
    psum x2 -> x0, waiting for transfers between devices: 96.8 us -> none  [the longest x1 55.6 us: per_device(): summed = lax.psum(expert_terms.astype(jnp.bfloat16), 'tp')]
    pallas_call x0 -> x1, Pallas kernels: none -> 63.3 us  [moe(): pl.pallas_call(moe_kernel, out_shape=jax.ShapeDtypeStruct((32, 512), BF),...]
    all_to_all x1 -> x0, blocking collectives: 35.8 us -> none  [per_device(): lax.all_to_all(sent, 'grp', split_axis=0, concat_axis=1, tiled=True)]
    all_to_all x1 -> x0, waiting for transfers between devices: 25.8 us -> none  [per_device(): lax.all_to_all(summed, 'grp', split_axis=1, concat_axis=0, tiled=True)]
    dot_general x9 -> x4, matrix products: 21.4 us -> 7.3 us  [dot(): return jnp.dot(a, b, preferred_element_type=F32)]
    unnamed x28 -> x14, local copies, waits for them, and re-layouts: 1.33 us -> 14.1 us
    all_to_all x3 -> x0, local copies, waits for them, and re-layouts: 10.1 us -> none  [the longest x2 6.55 us: per_device(): lax.all_to_all(sent, 'grp', split_axis=0, concat_axis=1, tiled=True)]
    all_to_all x1 -> x0, starting transfers between devices: 7.67 us -> none  [per_device(): lax.all_to_all(summed, 'grp', split_axis=1, concat_axis=0, tiled=True)]
  transfers between devices with their start and end apart: 3 -> 0, of which waited for: 3 -> 0; matrix products, arithmetic and copies ran while one was open for 3% -> 0% of each run, Pallas kernels for 0% -> 0%
where the time goes in v1:
time: 92.3 us; the launch traced here: 91.8 us
  Pallas kernels  63.3 us (69%)
  local copies, waits for them, and re-layouts  14.1 us (15%)
  matrix products  9.54 us (10%)
  other arithmetic  4.75 us (5%)
    pallas_call x1, Pallas kernels, moe(): pl.pallas_call(moe_kernel, out_shape=jax.ShapeDtypeStruct((32, 512), BF),...  63.3 us
    unnamed x14, local copies, waits for them, and re-layouts  14.1 us
    dot_general x4, matrix products, dot(): return jnp.dot(a, b, preferred_element_type=F32)  7.3 us

profile of v1, /device:TPU:0, one launch (start us, length us, event | category | flops | bytes accessed | tf_op | source)
XLA Modules:
  0.0 91.8 jit_solution(13889726337786434270)
XLA Ops:
  0.0 0.8 convert_element_type.47
  0.8 1.5 %fusion.18 = f32[32]{0:T(128)S(1)} fusion(bf16[32,2048]{1,0:T(8,128)(2,1)} %hidden.1), kind=kLoop, calls=%fused_computation.17 | loop fusion | flops 196576 | bytes 131200 | tf_op jit(solution)/shard_map/reduce_sum | solution.py:20
  2.3 1.4 %fusion.16 = f32[32,128]{1,0:T(8,128)S(1)} fusion(bf16[2048,128]{1,0:T(8,128)(2,1)} %param.22, bf16[32,2048]{1,0:T(8,128)(2,1)} %hidden.1, f32[2048]{0:T(1024)} %param.18, f32[32]{0:T(128)S(1)} %add_rsqrt_fusion.2), kind=kOutput, calls=%fused_computation.11 | convolution fusion | flops 17047552 | bytes 680064 | tf_op jit(solution)/shard_map/dot_general | solution.py:62
  3.7 0.7 iota_compare_fusion
  4.5 1.3 %multiply_reduce_fusion.1 = (f32[32]{0:T(128)S(1)}, f32[32,128]{1,0:T(8,128)S(1)}) fusion(bf16[2048,128]{1,0:T(8,128)(2,1)S(1)} %copy-done, bf16[32,2048]{1,0:T(8,128)(2,1)} %hidden.1, f32[2048]{0:T(1024)} %param.18, f32[32]{0:T(128)S(1)} %add_rsqrt_fusion.2), kind=kOutput, calls=%fused_computation.45 | convolution fusion | flops 17047520 | bytes 680192 | tf_op jit(solution)/shard_map/dot_general | solution.py:62
  5.8 0.7 multiply_bitcast_fusion
  6.5 0.1 fusion.37
  6.7 0.1 maximum_bitcast_fusion
  6.7 0.1 multiply_cosine_fusion.1
  6.9 3.2 %convolution_bitcast_fusion = f32[4,8,8,128]{3,1,2,0:T(8,128)S(1)} fusion(bf16[2048,1024]{1,0:T(8,128)(2,1)} %param.20, bf16[32,2048]{1,0:T(8,128)(2,1)} %hidden.1, f32[2048]{0:T(1024)} %param.18, f32[32]{0:T(128)S(1)} %add_rsqrt_fusion.2), kind=kOutput, calls=%fused_computation.8 | convolution fusion | flops 134479872 | bytes 4464768 | tf_op jit(solution)/shard_map/dot_general | solution.py:62
  10.1 0.1 multiply_reduce_fusion
  10.2 0.1 multiply_multiply_fusion
  10.3 0.1 subtract_convert_fusion
  10.4 0.2 fusion.33
  10.7 0.0 copy-done.1
  10.7 1.3 %fusion.45 = (f32[32,8]{1,0:T(8,128)S(1)}, f32[32,8,512]{2,1,0:T(8,128)S(1)}) fusion(bf16[32,1,512,128]{3,2,1,0:T(8,128)(2,1)S(1)} %copy-done.1, bf16[32,8,64]{2,1,0:T(8,128)(2,1)S(1)} %get-tuple-element.6, bf16[32,8,64]{2,1,0:T(8,128)(2,1)S(1)} %get-tuple-element.5, pred[32,512]{1,0:T(8,128)(4,1)S(1)} %iota_compare_fusion), kind=kOutput, calls=%fused_computation.61 | convolution fusion | flops 34078464 | bytes 4801536 | tf_op jit(solution)/shard_map/rkgd,rkpd->rkgp/dot_general | solution.py:40
  12.0 0.2 fusion.17
  12.3 0.7 fusion.13
  13.0 0.7 copy-done.3
  13.7 1.5 %convolution_convert_fusion.terms = bf16[32,2048]{1,0:T(8,128)(2,1)} fusion(bf16[1024,2048]{1,0:T(8,128)(2,1)S(1)} %copy-done.3, bf16[4,8,8,128]{3,2,1,0:T(8,128)(2,1)S(1)} %bitcast.41), kind=kOutput, calls=%fused_computation.4 | convolution fusion | flops 134283264 | bytes 4390912 | tf_op jit(solution)/shard_map/dot_general | solution.py:62
  15.2 6.0 %copy.18.wg_hbm = bf16[4,2048,192]{2,1,0:T(8,128)(2,1)} copy(bf16[4,2048,192]{1,2,0:T(8,128)(2,1)} %param.29) | data formatting | bytes 6291456 | tf_op args[12]
  21.2 6.0 %copy.19.wu_hbm = bf16[4,2048,192]{2,1,0:T(8,128)(2,1)} copy(bf16[4,2048,192]{1,2,0:T(8,128)(2,1)} %param.30) | data formatting | bytes 6291456 | tf_op args[13]
  27.1 63.3 %moe.1 = bf16[32,512]{1,0:T(8,128)(2,1)} custom-call(bf16[32,2048]{1,0:T(8,128)(2,1)} %convolution_convert_fusion.terms, bf16[32,2048]{1,0:T(8,128)(2,1)} %hidden.1, f32[1,2048]{1,0:T(1,128)} %bitcast.44, s32[8,32]{1,0:T(8,128)} %bitcast.45, bf16[2048,128]{1,0:T(8,128)(2,1)} %w_router.1, bf16[4,2048,192]{2,1,0:T(8,128)(2,1)} %copy.18.wg_hbm, ...), custom_call_target="tpu_custom_call" | custom-call | tf_op jit(solution)/shard_map/moe/pallas_call | solution.py:377
  90.4 1.4 %copy.31 = bf16[32,512]{1,0:T(8,128)(2,1)} copy(bf16[32,512]{1,0:T(8,128)(2,1)} %moe.1) | data formatting | bytes 65536
  (15 shorter events, 0.1 us)
Async XLA Ops:
  0.0 4.5 %copy-start = (bf16[2048,128]{1,0:T(8,128)(2,1)S(1)}, bf16[2048,128]{1,0:T(8,128)(2,1)}, u32[]{:S(2)}) copy-start(bf16[2048,128]{1,0:T(8,128)(2,1)} %param.21) | copy-start | bytes 1572868
  0.0 10.7 %copy-start.1 = (bf16[32,1,512,128]{3,2,1,0:T(8,128)(2,1)S(1)}, bf16[32,1,512,128]{3,2,1,0:T(8,128)(2,1)}, u32[]{:S(2)}) copy-start(bf16[32,1,512,128]{3,2,1,0:T(8,128)(2,1)} %param.25) | copy-start | bytes 12582916
  0.0 10.2 %copy-start.4 = (f32[128]{0:T(128)S(1)}, f32[128]{0:T(128)}, u32[]{:S(2)}) copy-start(f32[128]{0:T(128)} %param.23) | copy-start | bytes 1540
  10.0 2.2 %copy-start.2 = (bf16[32,1,512,128]{3,2,1,0:T(8,128)(2,1)S(1)}, bf16[32,1,512,128]{3,2,1,0:T(8,128)(2,1)}, u32[]{:S(2)}) copy-start(bf16[32,1,512,128]{3,2,1,0:T(8,128)(2,1)} %param.26) | copy-start | bytes 12582916
  10.7 3.0 %copy-start.3 = (bf16[1024,2048]{1,0:T(8,128)(2,1)S(1)}, bf16[1024,2048]{1,0:T(8,128)(2,1)}, u32[]{:S(2)}) copy-start(bf16[1024,2048]{1,0:T(8,128)(2,1)} %param.27) | copy-start | bytes 12582916

commit v2 on v0

v2 whole, which is shorter than its diff:
```python
import math

import jax
import jax.numpy as jnp
from jax import lax
from jax.experimental import pallas as pl
from jax.experimental.pallas import tpu as pltpu
from jax.sharding import PartitionSpec as P

rope_base = 1000000.0
norm_eps = 1e-06
MESH = pl.DeviceIdType.MESH
BF = jnp.bfloat16
F32 = jnp.float32

ORDER_A = ("x", "y", "z")
ORDER_B = ("y", "z", "x")
ORDER_C = ("z", "x", "y")


def dot(a, b):
    return jnp.dot(a, b, preferred_element_type=F32)


def dot_t(a, b):
    return lax.dot_general(a, b, (((1,), (1,)), ((), ())), preferred_element_type=F32)


def rms_scale(values, gain):
    return values * lax.rsqrt(jnp.mean(values * values, axis=-1, keepdims=True) + norm_eps) * gain


def coords():
    g = lax.axis_index("grp")
    return {"z": g // 8, "x": (g // 2) % 4, "c": g % 2, "y": lax.axis_index("tp")}


def device(co):
    return ((co["z"] * 4 + co["x"]) * 2 + co["c"], co["y"])


def moved(co, axis, d):
    size = 2 if axis == "c" else 4
    return dict(co, **{axis: (co[axis] + d + size) % size})


def block(ref, q, free, co, half=None):
    at = [slice(None) if a in free else co[a] for a in ("y", "z", "x")]
    if half is not None:
        first = [a in free for a in ("y", "z", "x")].index(True)
        at[first] = slice(2 * half, 2 * half + 2)
    return ref.at[q, co["c"], at[0], at[1], at[2]]


def quarter(v):
    return pl.ds(pl.multiple_of(v * 512, 512), 512)


def strips(ref, at, q):
    return jnp.concatenate([ref[(*at, slice(y * 512 + q * 128, y * 512 + q * 128 + 128))] for y in range(4)], axis=-1)


def layer_kernel(
    hidden_h, again_h, fgain_h, wq_h, wk_h, wv_h, qgain_h, kgain_h, kc_h, vc_h, wo_h, router_h,
    wg_h, wu_h, wd_h, len_h, ids_h,
    out_ref,
    hidden, again, fgain, wq, wk, wv, qgain, kgain, kc, vc, wo, router, wgu, wd, lens, ids,
    qs, att, kn, vn, terms, tin, ids_all, xa, sel, sel_t, msel, gu_acc, lg_acc, ya, ysib,
    r1u, r1, s1, r2, s2, r3, mid_ref,
    in_sem, kv_sem, wo_sem, ex_sem,
    t_send, t_recv, i_send, i_recv, g_send, g_recv, c_send, c_recv, e_send, e_recv, s_send, s_recv,
):
    co = coords()
    grp = lax.axis_index("grp")
    me_y = co["y"]
    me_c = co["c"]
    sibling = moved(co, "c", 1)

    def local(src, dst, sem):
        return pltpu.make_async_copy(src, dst, sem)

    def remote(src, dst, ss, rs, to):
        return pltpu.make_async_remote_copy(
            src_ref=src, dst_ref=dst, send_sem=ss, recv_sem=rs, device_id=device(to),
            device_id_type=MESH,
        )

    small = [
        local(s, d, in_sem.at[i])
        for i, (s, d) in enumerate(
            (
                (hidden_h, hidden), (again_h, again), (len_h, lens), (qgain_h, qgain),
                (kgain_h, kgain), (fgain_h, fgain), (ids_h, ids), (wk_h, wk), (wv_h, wv),
            )
        )
    ]
    wq_copies = [
        local(wq_h.at[:, i * 256 : (i + 1) * 256], wq.at[:, i * 256 : (i + 1) * 256], in_sem.at[9 + i])
        for i in range(4)
    ]

    def kv_copies(i):
        rows = pl.ds(i * 8, 8)
        return (
            local(kc_h.at[rows], kc.at[rows], kv_sem.at[0, i]),
            local(vc_h.at[rows], vc.at[rows], kv_sem.at[1, i]),
        )

    wo_order = (2, 1, 3, 0)

    def wo_copy(d):
        cols = quarter((me_y + d) % 4)
        return local(wo_h.at[:, cols], wo.at[d], wo_sem.at[d])

    expert_copies = [
        local(router_h, router, ex_sem.at[0]),
        local(wg_h, wgu.at[:, 0:192], ex_sem.at[1]),
        local(wu_h, wgu.at[:, 192:384], ex_sem.at[2]),
        local(wd_h, wd, ex_sem.at[3]),
    ]
    for cp in small + wq_copies:
        cp.start()
    for i in range(4):
        for cp in kv_copies(i):
            cp.start()
    for d in wo_order:
        wo_copy(d).start()

    bar = pltpu.get_barrier_semaphore()

    def greet(d, _):
        pl.semaphore_signal(bar, inc=1, device_id=((grp + d) % 32, me_y), device_id_type=MESH)
        return 0

    lax.fori_loop(1, 32, greet, 0)
    for d in (1, 2, 3):
        pl.semaphore_signal(bar, inc=1, device_id=device(moved(co, "y", d)), device_id_type=MESH)

    for cp in small[:7]:
        cp.wait()
    normed = rms_scale(hidden[...].astype(F32), again[...]).astype(BF)
    row32 = lax.broadcasted_iota(jnp.int32, (32, 128), 0)
    lane = lax.broadcasted_iota(jnp.int32, (32, 128), 1)
    position = jnp.zeros((32, 128), jnp.int32)
    for r in range(32):
        position = jnp.where(row32 == r, lens[r], position)
    steps_half = (lane % 64).astype(F32)
    angle = position.astype(F32) * jnp.exp(steps_half * (-2.0 / 128 * math.log(rope_base)))
    cosine = jnp.cos(angle)
    sine = jnp.sin(angle) * jnp.where(lane < 64, -1.0, 1.0)

    def rotate(values):
        return values * cosine + pltpu.roll(values, 64, 1) * sine

    small[7].wait()
    kn[...] = rotate(rms_scale(dot(normed, wk[...]), kgain[...])).astype(BF).astype(F32)
    small[8].wait()
    vn[...] = dot(normed, wv[...]).astype(BF).astype(F32)
    for i in range(4):
        wq_copies[i].wait()
        pair = dot(normed, wq[:, i * 256 : (i + 1) * 256])
        for j in (0, 1):
            qs[:, 2 * i + j, :] = rotate(rms_scale(pair[:, j * 128 : (j + 1) * 128], qgain[...]))

    lane8 = lax.broadcasted_iota(jnp.int32, (8, 128), 1)
    idv = ids[...]
    ids_all[grp] = jnp.where(lane8 // 32 == co["x"], jnp.concatenate([idv] * 4, axis=1), -1)
    pl.semaphore_wait(bar, 34)

    def ids_copy(d):
        return pltpu.make_async_remote_copy(
            src_ref=ids_all.at[grp], dst_ref=ids_all.at[grp], send_sem=i_send.at[d],
            recv_sem=i_recv.at[d], device_id=((grp + d) % 32, me_y), device_id_type=MESH,
        )

    def ids_start(d, _):
        ids_copy(d).start()
        return 0

    lax.fori_loop(1, 32, ids_start, 0)

    lane512 = lax.broadcasted_iota(jnp.int32, (8, 512), 1)
    scale = 128 ** -0.5

    def attend(i, _):
        for cp in kv_copies(i):
            cp.wait()
        scores, owns = [], []
        for j in range(8):
            r = i * 8 + j
            q = qs[r].astype(BF)
            s = dot_t(q, kc[r]) * scale
            scores.append(jnp.where(lane512 < lens[r], s, -jnp.inf))
            owns.append(jnp.sum(q.astype(F32) * kn[pl.ds(r, 1), :], axis=1, keepdims=True) * scale)
        s = jnp.concatenate(scores, axis=0)
        own = jnp.concatenate(owns, axis=0)
        top = jnp.maximum(jnp.max(s, axis=1, keepdims=True), own)
        ex = jnp.exp(s - top)
        ex_own = jnp.exp(own - top)
        denom = jnp.sum(ex, axis=1, keepdims=True) + ex_own
        probs = (ex / denom).astype(BF)
        probs_own = (ex_own / denom).astype(BF).astype(F32)
        for j in range(8):
            r = i * 8 + j
            rows = slice(j * 8, (j + 1) * 8)
            att[r] = dot(probs[rows], vc[r]) + probs_own[rows] * vn[pl.ds(r, 1), :]
        return 0

    lax.fori_loop(0, 4, attend, 0)
    for cp in expert_copies:
        cp.start()

    heads = jnp.concatenate([att[:, h, :].astype(BF) for h in range(8)], axis=1)

    def t_copy(d):
        return remote(terms.at[d - 1], tin.at[d - 1], t_send.at[d - 1], t_recv.at[d - 1], moved(co, "y", d))

    for d in wo_order[:3]:
        wo_copy(d).wait()
        terms[d - 1] = dot(heads, wo[d]).astype(BF)
        t_copy(d).start()
    wo_copy(0).wait()
    mid = hidden[:, quarter(me_y)].astype(F32) + dot(heads, wo[0]).astype(BF).astype(F32)
    for d in (1, 3, 2):
        t_copy(d).wait_recv()
        mid = mid + tin[d - 1].astype(F32)
    mid_ref[...] = mid
    sent = (mid * fgain[:, quarter(me_y)]).astype(BF)
    for q in range(4):
        xa[q, me_c, me_y, co["z"], co["x"]] = sent[:, q * 128 : (q + 1) * 128]

    def each_part(fn):
        fn(0, ORDER_A)
        fn(1, ORDER_B)
        fn(2, ORDER_C)
        last_part(fn)

    def last_part(fn):
        pl.when(me_c == 0)(lambda: fn(3, ORDER_A))
        pl.when(me_c == 1)(lambda: fn(3, ORDER_B))

    def gather(q, part, sem, to):
        return remote(part, part, g_send.at[q, sem], g_recv.at[q, sem], to)

    def stage1(q, order, d):
        return gather(q, block(xa, q, (), co), d - 1, moved(co, order[0], d))

    def stage2(q, order, d):
        return gather(q, block(xa, q, order[:1], co), 2 + d, moved(co, order[1], d))

    def piece(q, order, j, plane):
        at = moved(moved(co, order[1], -j), order[2], plane)
        return block(xa, q, order[:1], at)

    def stage3(q, order, j, way):
        return gather(q, piece(q, order, j, 0), (6 if way > 0 else 10) + j, moved(co, order[2], way))

    relay_way = {0: 1, 1: -1, 3: 1, 2: -1}
    piece_order = (0, 1, 3, 2)

    def relay(q, order, j):
        way = relay_way[j]
        return gather(q, piece(q, order, j, -way), 14 + j, moved(co, order[2], way))

    def over(q, order, plane):
        part = block(xa, q, order[:2], moved(co, order[2], plane))
        return remote(part, part, c_send.at[q, plane % 4], c_recv.at[q, plane % 4], sibling)

    def begin1(q, order):
        for d in (1, 3, 2):
            stage1(q, order, d).start()

    def begin2(q, order):
        for d in (1, 3, 2):
            stage1(q, order, d).wait_recv()
        for d in (1, 3, 2):
            stage2(q, order, d).start()
        stage3(q, order, 0, 1).start()
        stage3(q, order, 0, -1).start()

    def begin3(q, order):
        for j in piece_order[1:]:
            stage2(q, order, j).wait_recv()
            stage3(q, order, j, 1).start()
            stage3(q, order, j, -1).start()
        over(q, order, 0).start()

    def pass_on(q, order):
        for j in piece_order:
            way = relay_way[j]
            stage3(q, order, j, way).wait_recv()
            relay(q, order, j).start()

    def end_near(q, order):
        for j in piece_order:
            stage3(q, order, j, -relay_way[j]).wait_recv()
        over(q, order, -1).start()
        over(q, order, 1).start()

    def end_far(q, order):
        for j in piece_order:
            relay(q, order, j).wait_recv()
        over(q, order, 2).start()

    def end_over(q, order):
        for plane in (0, -1, 1, 2):
            over(q, order, plane).wait_recv()

    each_part(begin1)

    def ids_wait(d, _):
        ids_copy(d).wait()
        return 0

    lax.fori_loop(1, 32, ids_wait, 0)
    row = lax.broadcasted_iota(jnp.int32, (256, 256), 0)
    col = lax.broadcasted_iota(jnp.int32, (256, 256), 1)
    before = jnp.where((row < col) & (row // 32 == col // 32), 1.0, 0.0).astype(BF)
    lane256 = lax.broadcasted_iota(jnp.int32, (8, 256), 1)
    sub8 = lax.broadcasted_iota(jnp.int32, (8, 256), 0)
    sub32 = lax.broadcasted_iota(jnp.int32, (32, 256), 0)
    sub128 = lax.broadcasted_iota(jnp.int32, (128, 256), 0)

    def make_slots(z):
        halves = []
        for c in (0, 1):
            t = ids_all[z * 8 + c]
            for x in (1, 2, 3):
                t = jnp.maximum(t, ids_all[z * 8 + x * 2 + c])
            halves.append(t)
        idz = jnp.concatenate(halves, axis=1)
        picked = jnp.zeros((8, 256), F32)
        chosen = jnp.zeros((128, 256), F32)
        for k in range(8):
            row_k = idz[k : k + 1, :]
            picked = picked + jnp.where(row_k == grp * 4 + sub8, 1.0, 0.0)
            chosen = chosen + jnp.where(row_k == sub128, 1.0, 0.0)
        rank = dot(picked.astype(BF), before).astype(jnp.int32)
        place = jnp.where(picked > 0.5, (lane256 // 32) * 4 + rank, -1)
        mine = jnp.concatenate(
            [jnp.where(sub32 == place[e : e + 1, :], 1.0, 0.0) for e in range(4)], axis=0
        )
        sel[z] = mine.astype(BF)
        sel_t[z] = mine.T.astype(BF)
        ms = dot_t(mine.astype(BF), chosen.astype(BF))
        for e in range(4):
            msel[e, z * 32 : (z + 1) * 32, :] = ms[e * 32 : (e + 1) * 32]

    make_slots(0)
    each_part(begin2)
    make_slots(1)
    make_slots(2)
    each_part(begin3)
    make_slots(3)
    for cp in expert_copies:
        cp.wait()
    each_part(pass_on)
    each_part(end_near)

    inv_gain = 1.0 / fgain[...]
    squares = [None] * 4

    def products(q, first):
        rows_z = [
            dot(
                sel[z],
                jnp.concatenate(
                    [
                        jnp.concatenate([xa[q, c, y, z].reshape(128, 128) for c in (0, 1)], axis=0)
                        for y in range(4)
                    ],
                    axis=1,
                ),
            )
            for z in range(4)
        ]
        inv = jnp.concatenate(
            [inv_gain[:, y * 512 + q * 128 : y * 512 + q * 128 + 128] for y in range(4)], axis=1
        )
        w_r = jnp.concatenate(
            [router[y * 512 + q * 128 : y * 512 + q * 128 + 128, :] for y in range(4)], axis=0
        )
        for e in range(4):
            rows32 = jnp.concatenate([rows_z[z][e * 32 : (e + 1) * 32] for z in range(4)], axis=0)
            plain = rows32 * inv
            square = jnp.sum(plain * plain, axis=1, keepdims=True)
            rows = rows32.astype(BF)
            gu = dot_t(rows, strips(wgu, (e, slice(None)), q))
            lg = dot(rows, w_r)
            if first:
                squares[e] = square
                gu_acc[e] = gu
                lg_acc[e] = lg
            else:
                squares[e] = squares[e] + square
                gu_acc[e] = gu_acc[e] + gu
                lg_acc[e] = lg_acc[e] + lg

    end_far(0, ORDER_A)
    end_far(1, ORDER_B)
    end_far(2, ORDER_C)
    end_over(0, ORDER_A)
    products(0, True)
    last_part(end_far)
    end_over(1, ORDER_B)
    products(1, False)
    end_over(2, ORDER_C)
    products(2, False)
    last_part(end_over)
    products(3, False)

    lane128 = lax.broadcasted_iota(jnp.int32, (128, 128), 1)
    active, weight = [], []
    for e in range(4):
        norm = lax.rsqrt(squares[e] * (1.0 / 2048) + norm_eps)
        logits = lg_acc[e] * norm
        on = msel[e] > 0.5
        top = jnp.max(jnp.where(on, logits, -1e30), axis=1, keepdims=True)
        ex = jnp.where(on, jnp.exp(jnp.where(on, logits - top, 0.0)), 0.0)
        total = jnp.sum(ex, axis=1, keepdims=True)
        mine = jnp.sum(jnp.where(lane128 == grp * 4 + e, ex, 0.0), axis=1, keepdims=True)
        weight.append(mine / jnp.where(total > 0.0, total, 1.0))
        gate = gu_acc[e, :, 0:192] * norm
        upper = gu_acc[e, :, 192:384] * norm
        active.append((gate / (1.0 + jnp.exp(-gate)) * upper).astype(BF))

    def pair_copy(q):
        return remote(ya.at[q, 1 - me_c], ysib.at[q], e_send.at[q], e_recv.at[q], sibling)

    def token_sums(q):
        res = [(dot(active[e], strips(wd, (e, slice(None)), q)) * weight[e]).astype(BF) for e in range(4)]
        for z in range(4):
            slots = jnp.concatenate([res[e][z * 32 : (z + 1) * 32] for e in range(4)], axis=0)
            part = dot(sel_t[z], slots).astype(BF)
            for c in (0, 1):
                for y in range(4):
                    ya[q, c, y, z] = part[c * 128 : (c + 1) * 128, y * 128 : (y + 1) * 128].reshape(4, 32, 128)
        pair_copy(q).start()

    def scatter(q, src, dst, sem, to):
        return remote(src, dst, s_send.at[q, sem], s_recv.at[q, sem], to)

    def first(q, order, what, way):
        side = 0 if way > 0 else 1
        to = moved(co, order[2], way)
        if what == "far":
            src = block(ya, q, order[:2], moved(co, order[2], 2), side)
            return scatter(q, src, r1u.at[q, side], side, to)
        half = 1 - side if what == "near" else side
        src = block(ya, q, order[:2], to, half)
        return scatter(q, src, r1.at[q, side, 2 * half : 2 * half + 2], (2 if what == "near" else 4) + side, to)

    def left_axes(order):
        return [a for a in ("y", "z", "x") if a != order[2]]

    def second(q, order, d):
        axis = order[1]
        to = moved(co, axis, d)
        src = s1.at[q, to[axis]] if left_axes(order)[0] == axis else s1.at[q, :, to[axis]]
        return scatter(q, src, r2.at[q, d - 1], 5 + d, to)

    def third(q, order, d):
        to = moved(co, order[0], d)
        return scatter(q, s2.at[q, to[order[0]]], r3.at[q, d - 1], 8 + d, to)

    def scatter1(q, order):
        first(q, order, "far", 1).start()
        first(q, order, "far", -1).start()
        first(q, order, "near", 1).start()
        first(q, order, "near", -1).start()

    def pair_add(q):
        pair_copy(q).wait()
        own = ya.at[q, me_c]
        own[...] = (own[...].astype(F32) + ysib[q].astype(F32)).astype(BF)

    def scatter_relay(q, order):
        for way, side in ((1, 0), (-1, 1)):
            first(q, order, "far", way).wait_recv()
            mine = block(ya, q, order[:2], moved(co, order[2], way), side)
            mine[...] = (mine[...].astype(F32) + r1u[q, side].astype(F32)).astype(BF)
            first(q, order, "relayed", way).start()

    def scatter2(q, order):
        for way in (1, -1):
            first(q, order, "near", way).wait_recv()
            first(q, order, "relayed", way).wait_recv()
        own = block(ya, q, order[:2], co)[...].astype(F32)
        s1[q] = (own + r1[q, 0].astype(F32) + r1[q, 1].astype(F32)).astype(BF)
        for d in (1, 3, 2):
            second(q, order, d).start()

    def scatter3(q, order):
        for d in (1, 3, 2):
            second(q, order, d).wait_recv()
        own = s1[q, co[order[1]]] if left_axes(order)[0] == order[1] else s1[q, :, co[order[1]]]
        s2[q] = (
            own.astype(F32) + r2[q, 0].astype(F32) + r2[q, 1].astype(F32) + r2[q, 2].astype(F32)
        ).astype(BF)
        for d in (1, 3, 2):
            third(q, order, d).start()

    def finish(q, order):
        for d in (1, 3, 2):
            third(q, order, d).wait_recv()
        own = s2[q, co[order[0]]].astype(F32)
        cols = slice(q * 128, (q + 1) * 128)
        out_ref[:, cols] = (
            mid_ref[:, cols]
            + ((own + r3[q, 0].astype(F32)) + (r3[q, 1].astype(F32) + r3[q, 2].astype(F32)))
        ).astype(BF)

    token_sums(3)
    token_sums(0)
    pair_add(3)
    last_part(scatter1)
    token_sums(1)
    pair_add(0)
    scatter1(0, ORDER_A)
    token_sums(2)
    pair_add(1)
    scatter1(1, ORDER_B)
    last_part(scatter_relay)
    pair_add(2)
    scatter1(2, ORDER_C)

    def order_of_end(fn):
        last_part(fn)
        fn(0, ORDER_A)
        fn(1, ORDER_B)
        fn(2, ORDER_C)

    scatter_relay(0, ORDER_A)
    scatter_relay(1, ORDER_B)
    scatter_relay(2, ORDER_C)
    order_of_end(scatter2)
    order_of_end(scatter3)
    order_of_end(finish)

    for d in (1, 2, 3):
        t_copy(d).wait_send()

    def sent_all(q, order):
        for d in (1, 2, 3):
            stage1(q, order, d).wait_send()
            stage2(q, order, d).wait_send()
            second(q, order, d).wait_send()
            third(q, order, d).wait_send()
        for j in range(4):
            stage3(q, order, j, 1).wait_send()
            stage3(q, order, j, -1).wait_send()
            relay(q, order, j).wait_send()
        for plane in (0, -1, 1, 2):
            over(q, order, plane).wait_send()
        for way in (1, -1):
            for what in ("far", "near", "relayed"):
                first(q, order, what, way).wait_send()

    each_part(sent_all)


def per_device(
    hidden_in, attn_gain, ffn_gain, w_query, w_key, w_value, q_gain, k_gain, key_cache,
    value_cache, w_out, w_router, w_gate, w_up, w_down, cache_len, expert_ids,
):
    hbm = pl.BlockSpec(memory_space=pl.ANY)
    dma = pltpu.SemaphoreType.DMA
    vmem = pltpu.VMEM
    return pl.pallas_call(
        layer_kernel,
        out_shape=jax.ShapeDtypeStruct((32, 512), BF),
        in_specs=[hbm] * 17,
        out_specs=pl.BlockSpec(memory_space=pltpu.VMEM),
        scratch_shapes=[
            vmem((32, 2048), BF), vmem((1, 2048), F32), vmem((1, 2048), F32), vmem((2048, 1024), BF),
            vmem((2048, 128), BF), vmem((2048, 128), BF), vmem((1, 128), F32), vmem((1, 128), F32),
            vmem((32, 512, 128), BF), vmem((32, 512, 128), BF), vmem((4, 1024, 512), BF),
            vmem((2048, 128), BF), vmem((4, 384, 2048), BF), vmem((4, 192, 2048), BF),
            pltpu.SMEM((32,), jnp.int32), vmem((8, 32), jnp.int32),
            vmem((32, 8, 128), F32), vmem((32, 8, 128), F32), vmem((32, 128), F32), vmem((32, 128), F32),
            vmem((3, 32, 512), BF), vmem((3, 32, 512), BF), vmem((32, 8, 128), jnp.int32),
            vmem((4, 2, 4, 4, 4, 32, 128), BF), vmem((4, 128, 256), BF), vmem((4, 256, 128), BF),
            vmem((4, 128, 128), F32), vmem((4, 128, 384), F32), vmem((4, 128, 128), F32),
            vmem((4, 2, 4, 4, 4, 32, 128), BF), vmem((4, 4, 4, 4, 32, 128), BF),
            vmem((4, 2, 2, 4, 32, 128), BF), vmem((4, 2, 4, 4, 32, 128), BF), vmem((4, 4, 4, 32, 128), BF),
            vmem((4, 3, 4, 32, 128), BF), vmem((4, 4, 32, 128), BF), vmem((4, 3, 32, 128), BF),
            vmem((32, 512), F32),
            dma((13,)), dma((2, 4)), dma((4,)), dma((4,)),
            dma((3,)), dma((3,)), dma((32,)), dma((32,)), dma((4, 18)), dma((4, 18)),
            dma((4, 4)), dma((4, 4)), dma((4,)), dma((4,)), dma((4, 12)), dma((4, 12)),
        ],
        compiler_params=pltpu.CompilerParams(
            collective_id=0, has_side_effects=True, vmem_limit_bytes=58 << 20
        ),
        name="layer",
    )(
        hidden_in, attn_gain.reshape(1, -1), ffn_gain.reshape(1, -1), w_query, w_key, w_value,
        q_gain.reshape(1, -1), k_gain.reshape(1, -1), key_cache.reshape(32, 512, 128),
        value_cache.reshape(32, 512, 128), w_out, w_router, w_gate.swapaxes(1, 2),
        w_up.swapaxes(1, 2), w_down, cache_len, expert_ids.T,
    )


def solution(mesh):
    in_specs = (
        P("grp", None), P(), P(), P(None, "tp"), P(None, "tp"), P(None, "tp"), P(), P(),
        P("grp", "tp", None, None), P("grp", "tp", None, None), P("tp", None), P(),
        P("grp", None, "tp"), P("grp", None, "tp"), P("grp", "tp", None), P("grp"), P("grp", None),
    )
    return jax.shard_map(
        per_device, mesh=mesh, in_specs=in_specs, out_specs=P("grp", "tp"), check_vma=False
    )
```

time: 238 us -> 67.6 us (0.28)
  waiting for transfers between devices: 123 us -> 0 us
  Pallas kernels: 0 us -> 66 us
  blocking collectives: 35.8 us -> 0 us
  local copies, waits for them, and re-layouts: 27.2 us -> 1.38 us
  matrix products: 23.6 us -> 0 us
  between operations: 13.7 us -> 0.01 us
  starting transfers between devices: 7.75 us -> 0 us
  other arithmetic: 6.54 us -> 0 us
    psum x2 -> x0, waiting for transfers between devices: 96.8 us -> none  [the longest x1 55.6 us: per_device(): summed = lax.psum(expert_terms.astype(jnp.bfloat16), 'tp')]
    pallas_call x0 -> x1, Pallas kernels: none -> 66 us  [per_device(): pl.pallas_call(layer_kernel, out_shape=jax.ShapeDtypeStruct((32, 512), BF...]
    all_to_all x1 -> x0, blocking collectives: 35.8 us -> none  [per_device(): lax.all_to_all(sent, 'grp', split_axis=0, concat_axis=1, tiled=True)]
    all_to_all x1 -> x0, waiting for transfers between devices: 25.8 us -> none  [per_device(): lax.all_to_all(summed, 'grp', split_axis=1, concat_axis=0, tiled=True)]
    dot_general x12 -> x0, matrix products: 23.6 us -> none  [the longest x1 5.38 us: per_device(): jnp.einsum('esf,efd->esd', active, w_down, preferred_element_type=jnp.flo...]
    all_to_all x3 -> x0, local copies, waits for them, and re-layouts: 10.1 us -> none  [the longest x2 6.55 us: per_device(): lax.all_to_all(sent, 'grp', split_axis=0, concat_axis=1, tiled=True)]
    all_to_all x1 -> x0, starting transfers between devices: 7.67 us -> none  [per_device(): lax.all_to_all(summed, 'grp', split_axis=1, concat_axis=0, tiled=True)]
    reshape x2 -> x0, local copies, waits for them, and re-layouts: 6.07 us -> none  [the longest x1 4.12 us: per_device(): place_rows(targets, ffn_in, experts_all * capacity)]
  transfers between devices with their start and end apart: 3 -> 0, of which waited for: 3 -> 0; matrix products, arithmetic and copies ran while one was open for 3% -> 0% of each run, Pallas kernels for 0% -> 0%
where the time goes in v2:
time: 67.6 us; the launch traced here: 67.4 us
  Pallas kernels  66 us (98%)
  local copies, waits for them, and re-layouts  1.38 us (2%)
    pallas_call x1, Pallas kernels, per_device(): pl.pallas_call(layer_kernel, out_shape=jax.ShapeDtypeStruct((32, 512), BF...  66 us
    unnamed x1, local copies, waits for them, and re-layouts  1.38 us

profile of v2, /device:TPU:0, one launch (start us, length us, event | category | flops | bytes accessed | tf_op | source)
XLA Modules:
  0.0 67.4 jit_solution(6120911912418920222)
XLA Ops:
  0.0 66.0 %layer.1 = bf16[32,512]{1,0:T(8,128)(2,1)} custom-call(bf16[32,2048]{1,0:T(8,128)(2,1)} %hidden_h.1, f32[1,2048]{1,0:T(1,128)} %bitcast.13, f32[1,2048]{1,0:T(1,128)} %bitcast.14, bf16[2048,1024]{1,0:T(8,128)(2,1)} %wq_h.1, bf16[2048,128]{1,0:T(8,128)(2,1)} %wk_h.1, bf16[2048,128]{1,0:T(8,128)(2,1)} %wv_h.1, f32[1,128]{1,0:T(1,128)} %bitcast.16, ...), custom_call_target="tpu_custom_call" | custom-call | tf_op jit(solution)/shard_map/layer/pallas_call | solution.py:569
  66.1 1.4 %copy.19 = bf16[32,512]{1,0:T(8,128)(2,1)} copy(bf16[32,512]{1,0:T(8,128)(2,1)} %layer.1) | data formatting | bytes 65536

commit v3 on v2

--- a/solution.py
+++ b/solution.py
@@ -66,9 +66,9 @@
     out_ref,
     hidden, again, fgain, wq, wk, wv, qgain, kgain, kc, vc, wo, router, wgu, wd, lens, ids,
     qs, att, kn, vn, terms, tin, ids_all, xa, sel, sel_t, msel, gu_acc, lg_acc, ya, ysib,
-    r1u, r1, s1, r2, s2, r3, mid_ref,
+    r1u, r1, s1, r2, mid_ref, tally,
     in_sem, kv_sem, wo_sem, ex_sem,
-    t_send, t_recv, i_send, i_recv, g_send, g_recv, c_send, c_recv, e_send, e_recv, s_send, s_recv,
+    t_send, t_recv, i_send, i_recv, g_send, g_recv, c_recv, e_send, e_recv, s_send, s_recv,
 ):
     co = coords()
     grp = lax.axis_index("grp")
@@ -89,18 +89,18 @@
         local(s, d, in_sem.at[i])
         for i, (s, d) in enumerate(
             (
-                (hidden_h, hidden), (again_h, again), (len_h, lens), (qgain_h, qgain),
+                (len_h, lens), (hidden_h, hidden), (again_h, again), (qgain_h, qgain),
                 (kgain_h, kgain), (fgain_h, fgain), (ids_h, ids), (wk_h, wk), (wv_h, wv),
             )
         )
     ]
     wq_copies = [
-        local(wq_h.at[:, i * 256 : (i + 1) * 256], wq.at[:, i * 256 : (i + 1) * 256], in_sem.at[9 + i])
-        for i in range(4)
+        local(wq_h.at[:, i * 512 : (i + 1) * 512], wq.at[:, i * 512 : (i + 1) * 512], in_sem.at[9 + i])
+        for i in range(2)
     ]
 
     def kv_copies(i):
-        rows = pl.ds(i * 8, 8)
+        rows = slice(i * 16, (i + 1) * 16)
         return (
             local(kc_h.at[rows], kc.at[rows], kv_sem.at[0, i]),
             local(vc_h.at[rows], vc.at[rows], kv_sem.at[1, i]),
@@ -120,7 +120,7 @@
     ]
     for cp in small + wq_copies:
         cp.start()
-    for i in range(4):
+    for i in range(2):
         for cp in kv_copies(i):
             cp.start()
     for d in wo_order:
@@ -136,9 +136,7 @@
     for d in (1, 2, 3):
         pl.semaphore_signal(bar, inc=1, device_id=device(moved(co, "y", d)), device_id_type=MESH)
 
-    for cp in small[:7]:
-        cp.wait()
-    normed = rms_scale(hidden[...].astype(F32), again[...]).astype(BF)
+    small[0].wait()
     row32 = lax.broadcasted_iota(jnp.int32, (32, 128), 0)
     lane = lax.broadcasted_iota(jnp.int32, (32, 128), 1)
     position = jnp.zeros((32, 128), jnp.int32)
@@ -152,15 +150,21 @@
     def rotate(values):
         return values * cosine + pltpu.roll(values, 64, 1) * sine
 
+    for cp in small[1:7]:
+        cp.wait()
+    normed = rms_scale(hidden[...].astype(F32), again[...]).astype(BF)
     small[7].wait()
-    kn[...] = rotate(rms_scale(dot(normed, wk[...]), kgain[...])).astype(BF).astype(F32)
     small[8].wait()
+    keys = dot(normed, wk[...])
     vn[...] = dot(normed, wv[...]).astype(BF).astype(F32)
-    for i in range(4):
-        wq_copies[i].wait()
-        pair = dot(normed, wq[:, i * 256 : (i + 1) * 256])
-        for j in (0, 1):
-            qs[:, 2 * i + j, :] = rotate(rms_scale(pair[:, j * 128 : (j + 1) * 128], qgain[...]))
+    wq_copies[0].wait()
+    q_low = dot(normed, wq[:, 0:512])
+    wq_copies[1].wait()
+    q_high = dot(normed, wq[:, 512:1024])
+    kn[...] = rotate(rms_scale(keys, kgain[...])).astype(BF).astype(F32)
+    for h in range(8):
+        head = (q_low if h < 4 else q_high)[:, (h % 4) * 128 : (h % 4 + 1) * 128]
+        qs[:, h, :] = rotate(rms_scale(head, qgain[...])).astype(BF).astype(F32)
 
     lane8 = lax.broadcasted_iota(jnp.int32, (8, 128), 1)
     idv = ids[...]
@@ -169,8 +173,8 @@
 
     def ids_copy(d):
         return pltpu.make_async_remote_copy(
-            src_ref=ids_all.at[grp], dst_ref=ids_all.at[grp], send_sem=i_send.at[d],
-            recv_sem=i_recv.at[d], device_id=((grp + d) % 32, me_y), device_id_type=MESH,
+            src_ref=ids_all.at[grp], dst_ref=ids_all.at[grp], send_sem=i_send,
+            recv_sem=i_recv, device_id=((grp + d) % 32, me_y), device_id_type=MESH,
         )
 
     def ids_start(d, _):
@@ -179,41 +183,46 @@
 
     lax.fori_loop(1, 32, ids_start, 0)
 
-    lane512 = lax.broadcasted_iota(jnp.int32, (8, 512), 1)
     scale = 128 ** -0.5
-
-    def attend(i, _):
-        for cp in kv_copies(i):
-            cp.wait()
-        scores, owns = [], []
-        for j in range(8):
-            r = i * 8 + j
-            q = qs[r].astype(BF)
-            s = dot_t(q, kc[r]) * scale
-            scores.append(jnp.where(lane512 < lens[r], s, -jnp.inf))
-            owns.append(jnp.sum(q.astype(F32) * kn[pl.ds(r, 1), :], axis=1, keepdims=True) * scale)
-        s = jnp.concatenate(scores, axis=0)
-        own = jnp.concatenate(owns, axis=0)
-        top = jnp.maximum(jnp.max(s, axis=1, keepdims=True), own)
+    lane_request = lax.broadcasted_iota(jnp.int32, (128, 128), 1) // 8
+    where_p = lax.broadcasted_iota(jnp.int32, (512, 128), 0)
+
+    def spread(ref, i):
+        rows = ref[i * 16 : (i + 1) * 16]
+        return jnp.broadcast_to(rows[:, None, :], (16, 8, 128)).reshape(128, 128)
+
+    for i in range(2):
+        q = qs[i * 16 : (i + 1) * 16].reshape(128, 128)
+        q_t = q.T
+        own = jnp.sum((q * spread(kn, i)).T, axis=0, keepdims=True) * scale
+        weights = jnp.concatenate(
+            [jnp.where(lane_request == j, q_t, 0.0).astype(BF) for j in range(16)], axis=0
+        )
+        length = jnp.zeros((1, 128), jnp.int32)
+        for j in range(16):
+            length = jnp.where(lane_request[0:1] == j, lens[i * 16 + j], length)
+        kv_copies(i)[0].wait()
+        keys_all = jnp.concatenate([kc[i * 16 + j] for j in range(16)], axis=1)
+        s = dot(keys_all, weights) * scale
+        s = jnp.where(where_p < length, s, -jnp.inf)
+        top = jnp.maximum(jnp.max(s, axis=0, keepdims=True), own)
         ex = jnp.exp(s - top)
         ex_own = jnp.exp(own - top)
-        denom = jnp.sum(ex, axis=1, keepdims=True) + ex_own
-        probs = (ex / denom).astype(BF)
+        denom = jnp.sum(ex, axis=0, keepdims=True) + ex_own
+        probs = (ex / denom).T
         probs_own = (ex_own / denom).astype(BF).astype(F32)
-        for j in range(8):
-            r = i * 8 + j
-            rows = slice(j * 8, (j + 1) * 8)
-            att[r] = dot(probs[rows], vc[r]) + probs_own[rows] * vn[pl.ds(r, 1), :]
-        return 0
-
-    lax.fori_loop(0, 4, attend, 0)
+        own_terms = jnp.broadcast_to(probs_own, (128, 128)).T * spread(vn, i)
+        kv_copies(i)[1].wait()
+        rows = [dot(probs[j * 8 : (j + 1) * 8].astype(BF), vc[i * 16 + j]) for j in range(16)]
+        att[i * 16 : (i + 1) * 16] = (jnp.concatenate(rows, axis=0) + own_terms).reshape(16, 8, 128)
+
     for cp in expert_copies:
         cp.start()
 
     heads = jnp.concatenate([att[:, h, :].astype(BF) for h in range(8)], axis=1)
 
     def t_copy(d):
-        return remote(terms.at[d - 1], tin.at[d - 1], t_send.at[d - 1], t_recv.at[d - 1], moved(co, "y", d))
+        return remote(terms.at[d - 1], tin.at[d - 1], t_send, t_recv.at[d - 1], moved(co, "y", d))
 
     for d in wo_order[:3]:
         wo_copy(d).wait()
@@ -239,80 +248,73 @@
         pl.when(me_c == 0)(lambda: fn(3, ORDER_A))
         pl.when(me_c == 1)(lambda: fn(3, ORDER_B))
 
+    def chunks(n):
+        return tally.at[0:n]
+
+    def await_chunks(n, sem):
+        pltpu.make_async_copy(chunks(n), chunks(n), sem).wait()
+
     def gather(q, part, sem, to):
-        return remote(part, part, g_send.at[q, sem], g_recv.at[q, sem], to)
-
-    def stage1(q, order, d):
-        return gather(q, block(xa, q, (), co), d - 1, moved(co, order[0], d))
-
-    def stage2(q, order, d):
-        return gather(q, block(xa, q, order[:1], co), 2 + d, moved(co, order[1], d))
+        return remote(part, part, g_send.at[q], g_recv.at[q, sem], to)
+
+    def in_plane(q, order, i, j):
+        to = moved(moved(co, order[0], i), order[1], j)
+        return gather(q, block(xa, q, (), co), j, to)
 
     def piece(q, order, j, plane):
         at = moved(moved(co, order[1], -j), order[2], plane)
         return block(xa, q, order[:1], at)
 
-    def stage3(q, order, j, way):
-        return gather(q, piece(q, order, j, 0), (6 if way > 0 else 10) + j, moved(co, order[2], way))
-
     relay_way = {0: 1, 1: -1, 3: 1, 2: -1}
     piece_order = (0, 1, 3, 2)
 
+    def along(q, order, j, way):
+        sem = 4 + j if way == relay_way[j] else 8
+        return gather(q, piece(q, order, j, 0), sem, moved(co, order[2], way))
+
     def relay(q, order, j):
         way = relay_way[j]
-        return gather(q, piece(q, order, j, -way), 14 + j, moved(co, order[2], way))
+        return gather(q, piece(q, order, j, -way), 9, moved(co, order[2], way))
 
     def over(q, order, plane):
         part = block(xa, q, order[:2], moved(co, order[2], plane))
-        return remote(part, part, c_send.at[q, plane % 4], c_recv.at[q, plane % 4], sibling)
-
-    def begin1(q, order):
-        for d in (1, 3, 2):
-            stage1(q, order, d).start()
-
-    def begin2(q, order):
-        for d in (1, 3, 2):
-            stage1(q, order, d).wait_recv()
-        for d in (1, 3, 2):
-            stage2(q, order, d).start()
-        stage3(q, order, 0, 1).start()
-        stage3(q, order, 0, -1).start()
-
-    def begin3(q, order):
-        for j in piece_order[1:]:
-            stage2(q, order, j).wait_recv()
-            stage3(q, order, j, 1).start()
-            stage3(q, order, j, -1).start()
+        return remote(part, part, g_send.at[q], c_recv.at[q], sibling)
+
+    def begin(q, order):
+        for j in (2, 1, 3, 0):
+            for i in (2, 1, 3, 0):
+                if i or j:
+                    in_plane(q, order, i, j).start()
+
+    def begin_axis(q, order):
+        for j in piece_order:
+            await_chunks(4 if j else 3, g_recv.at[q, j])
+            along(q, order, j, 1).start()
+            along(q, order, j, -1).start()
         over(q, order, 0).start()
 
     def pass_on(q, order):
         for j in piece_order:
-            way = relay_way[j]
-            stage3(q, order, j, way).wait_recv()
+            along(q, order, j, relay_way[j]).wait_recv()
             relay(q, order, j).start()
 
     def end_near(q, order):
-        for j in piece_order:
-            stage3(q, order, j, -relay_way[j]).wait_recv()
+        await_chunks(16, g_recv.at[q, 8])
         over(q, order, -1).start()
         over(q, order, 1).start()
 
     def end_far(q, order):
-        for j in piece_order:
-            relay(q, order, j).wait_recv()
+        await_chunks(16, g_recv.at[q, 9])
         over(q, order, 2).start()
 
     def end_over(q, order):
-        for plane in (0, -1, 1, 2):
-            over(q, order, plane).wait_recv()
-
-    each_part(begin1)
-
-    def ids_wait(d, _):
-        ids_copy(d).wait()
-        return 0
-
-    lax.fori_loop(1, 32, ids_wait, 0)
+        await_chunks(64, c_recv.at[q])
+
+    each_part(begin)
+
+    others = ids_all.at[0:31]
+    pltpu.make_async_copy(others, others, i_recv).wait()
+    pltpu.make_async_copy(others, others, i_send).wait()
     row = lax.broadcasted_iota(jnp.int32, (256, 256), 0)
     col = lax.broadcasted_iota(jnp.int32, (256, 256), 1)
     before = jnp.where((row < col) & (row // 32 == col // 32), 1.0, 0.0).astype(BF)
@@ -347,11 +349,10 @@
             msel[e, z * 32 : (z + 1) * 32, :] = ms[e * 32 : (e + 1) * 32]
 
     make_slots(0)
-    each_part(begin2)
     make_slots(1)
     make_slots(2)
-    each_part(begin3)
     make_slots(3)
+    each_part(begin_axis)
     for cp in expert_copies:
         cp.wait()
     each_part(pass_on)
@@ -425,7 +426,7 @@
         active.append((gate / (1.0 + jnp.exp(-gate)) * upper).astype(BF))
 
     def pair_copy(q):
-        return remote(ya.at[q, 1 - me_c], ysib.at[q], e_send.at[q], e_recv.at[q], sibling)
+        return remote(ya.at[q, 1 - me_c], ysib.at[q], e_send, e_recv.at[q], sibling)
 
     def token_sums(q):
         res = [(dot(active[e], strips(wd, (e, slice(None)), q)) * weight[e]).astype(BF) for e in range(4)]
@@ -438,7 +439,7 @@
         pair_copy(q).start()
 
     def scatter(q, src, dst, sem, to):
-        return remote(src, dst, s_send.at[q, sem], s_recv.at[q, sem], to)
+        return remote(src, dst, s_send.at[q], s_recv.at[q, sem], to)
 
     def first(q, order, what, way):
         side = 0 if way > 0 else 1
@@ -448,20 +449,15 @@
             return scatter(q, src, r1u.at[q, side], side, to)
         half = 1 - side if what == "near" else side
         src = block(ya, q, order[:2], to, half)
-        return scatter(q, src, r1.at[q, side, 2 * half : 2 * half + 2], (2 if what == "near" else 4) + side, to)
+        return scatter(q, src, r1.at[q, side, 2 * half : 2 * half + 2], 2, to)
 
     def left_axes(order):
         return [a for a in ("y", "z", "x") if a != order[2]]
 
-    def second(q, order, d):
-        axis = order[1]
-        to = moved(co, axis, d)
-        src = s1.at[q, to[axis]] if left_axes(order)[0] == axis else s1.at[q, :, to[axis]]
-        return scatter(q, src, r2.at[q, d - 1], 5 + d, to)
-
-    def third(q, order, d):
-        to = moved(co, order[0], d)
-        return scatter(q, s2.at[q, to[order[0]]], r3.at[q, d - 1], 8 + d, to)
+    def second(q, order, i, j):
+        a, b = left_axes(order)
+        to = moved(moved(co, a, i), b, j)
+        return scatter(q, s1.at[q, to[a], to[b]], r2.at[q, i * 4 + j - 1], 3, to)
 
     def scatter1(q, order):
         first(q, order, "far", 1).start()
@@ -470,7 +466,7 @@
         first(q, order, "near", -1).start()
 
     def pair_add(q):
-        pair_copy(q).wait()
+        pair_copy(q).wait_recv()
         own = ya.at[q, me_c]
         own[...] = (own[...].astype(F32) + ysib[q].astype(F32)).astype(BF)
 
@@ -482,33 +478,22 @@
             first(q, order, "relayed", way).start()
 
     def scatter2(q, order):
-        for way in (1, -1):
-            first(q, order, "near", way).wait_recv()
-            first(q, order, "relayed", way).wait_recv()
+        pltpu.make_async_copy(r1.at[q], r1.at[q], s_recv.at[q, 2]).wait()
         own = block(ya, q, order[:2], co)[...].astype(F32)
         s1[q] = (own + r1[q, 0].astype(F32) + r1[q, 1].astype(F32)).astype(BF)
-        for d in (1, 3, 2):
-            second(q, order, d).start()
-
-    def scatter3(q, order):
-        for d in (1, 3, 2):
-            second(q, order, d).wait_recv()
-        own = s1[q, co[order[1]]] if left_axes(order)[0] == order[1] else s1[q, :, co[order[1]]]
-        s2[q] = (
-            own.astype(F32) + r2[q, 0].astype(F32) + r2[q, 1].astype(F32) + r2[q, 2].astype(F32)
-        ).astype(BF)
-        for d in (1, 3, 2):
-            third(q, order, d).start()
+        for j in (2, 1, 3, 0):
+            for i in (2, 1, 3, 0):
+                if i or j:
+                    second(q, order, i, j).start()
 
     def finish(q, order):
-        for d in (1, 3, 2):
-            third(q, order, d).wait_recv()
-        own = s2[q, co[order[0]]].astype(F32)
+        pltpu.make_async_copy(r2.at[q], r2.at[q], s_recv.at[q, 3]).wait()
+        a, b = left_axes(order)
+        total = s1[q, co[a], co[b]].astype(F32)
+        for n in range(15):
+            total = total + r2[q, n].astype(F32)
         cols = slice(q * 128, (q + 1) * 128)
-        out_ref[:, cols] = (
-            mid_ref[:, cols]
-            + ((own + r3[q, 0].astype(F32)) + (r3[q, 1].astype(F32) + r3[q, 2].astype(F32)))
-        ).astype(BF)
+        out_ref[:, cols] = (mid_ref[:, cols] + total).astype(BF)
 
     token_sums(3)
     token_sums(0)
@@ -534,29 +519,14 @@
     scatter_relay(1, ORDER_B)
     scatter_relay(2, ORDER_C)
     order_of_end(scatter2)
-    order_of_end(scatter3)
     order_of_end(finish)
 
-    for d in (1, 2, 3):
-        t_copy(d).wait_send()
-
-    def sent_all(q, order):
-        for d in (1, 2, 3):
-            stage1(q, order, d).wait_send()
-            stage2(q, order, d).wait_send()
-            second(q, order, d).wait_send()
-            third(q, order, d).wait_send()
-        for j in range(4):
-            stage3(q, order, j, 1).wait_send()
-            stage3(q, order, j, -1).wait_send()
-            relay(q, order, j).wait_send()
-        for plane in (0, -1, 1, 2):
-            over(q, order, plane).wait_send()
-        for way in (1, -1):
-            for what in ("far", "near", "relayed"):
-                first(q, order, what, way).wait_send()
-
-    each_part(sent_all)
+    pltpu.make_async_copy(tin, tin, t_send).wait()
+
+    pltpu.make_async_copy(ysib, ysib, e_send).wait()
+    for q in range(4):
+        await_chunks(127, g_send.at[q])
+        await_chunks(63, s_send.at[q])
 
 
 def per_device(
@@ -583,11 +553,11 @@
             vmem((4, 128, 128), F32), vmem((4, 128, 384), F32), vmem((4, 128, 128), F32),
             vmem((4, 2, 4, 4, 4, 32, 128), BF), vmem((4, 4, 4, 4, 32, 128), BF),
             vmem((4, 2, 2, 4, 32, 128), BF), vmem((4, 2, 4, 4, 32, 128), BF), vmem((4, 4, 4, 32, 128), BF),
-            vmem((4, 3, 4, 32, 128), BF), vmem((4, 4, 32, 128), BF), vmem((4, 3, 32, 128), BF),
-            vmem((32, 512), F32),
-            dma((13,)), dma((2, 4)), dma((4,)), dma((4,)),
-            dma((3,)), dma((3,)), dma((32,)), dma((32,)), dma((4, 18)), dma((4, 18)),
-            dma((4, 4)), dma((4, 4)), dma((4,)), dma((4,)), dma((4, 12)), dma((4, 12)),
+            vmem((4, 15, 32, 128), BF),
+            vmem((32, 512), F32), vmem((127, 32, 128), BF),
+            dma((11,)), dma((2, 2)), dma((4,)), dma((4,)),
+            dma, dma((3,)), dma, dma, dma((4,)), dma((4, 10)), dma((4,)), dma, dma((4,)),
+            dma((4,)), dma((4, 4)),
         ],
         compiler_params=pltpu.CompilerParams(
             collective_id=0, has_side_effects=True, vmem_limit_bytes=58 << 20

time: 67.6 us -> 62.3 us (0.922)
  Pallas kernels: 66 us -> 60.2 us
    pallas_call x1, Pallas kernels: 66 us -> 60.2 us  [per_device(): pl.pallas_call(layer_kernel, out_shape=jax.ShapeDtypeStruct((32, 512), BF...]
where the time goes in v3:
time: 62.3 us; the launch traced here: 61.6 us
  Pallas kernels  60.2 us (97%)
  local copies, waits for them, and re-layouts  1.38 us (2%)
    pallas_call x1, Pallas kernels, per_device(): pl.pallas_call(layer_kernel, out_shape=jax.ShapeDtypeStruct((32, 512), BF...  60.2 us
    unnamed x1, local copies, waits for them, and re-layouts  1.38 us

profile of v3, /device:TPU:0, one launch (start us, length us, event | category | flops | bytes accessed | tf_op | source)
XLA Modules:
  0.0 61.6 jit_solution(14991341825158368934)
XLA Ops:
  0.0 60.2 %layer.1 = bf16[32,512]{1,0:T(8,128)(2,1)} custom-call(bf16[32,2048]{1,0:T(8,128)(2,1)} %hidden_h.1, f32[1,2048]{1,0:T(1,128)} %bitcast.13, f32[1,2048]{1,0:T(1,128)} %bitcast.14, bf16[2048,1024]{1,0:T(8,128)(2,1)} %wq_h.1, bf16[2048,128]{1,0:T(8,128)(2,1)} %wk_h.1, bf16[2048,128]{1,0:T(8,128)(2,1)} %wv_h.1, f32[1,128]{1,0:T(1,128)} %bitcast.16, ...), custom_call_target="tpu_custom_call" | custom-call | tf_op jit(solution)/shard_map/layer/pallas_call | solution.py:539
  60.3 1.4 %copy.19 = bf16[32,512]{1,0:T(8,128)(2,1)} copy(bf16[32,512]{1,0:T(8,128)(2,1)} %layer.1) | data formatting | bytes 65536

commit v4 on v3

--- a/solution.py
+++ b/solution.py
@@ -120,11 +120,7 @@
     ]
     for cp in small + wq_copies:
         cp.start()
-    for i in range(2):
-        for cp in kv_copies(i):
-            cp.start()
-    for d in wo_order:
-        wo_copy(d).start()
+    kv_copies(0)[0].start()
 
     bar = pltpu.get_barrier_semaphore()
 
@@ -158,8 +154,13 @@
     keys = dot(normed, wk[...])
     vn[...] = dot(normed, wv[...]).astype(BF).astype(F32)
     wq_copies[0].wait()
+    kv_copies(0)[1].start()
+    kv_copies(1)[0].start()
     q_low = dot(normed, wq[:, 0:512])
     wq_copies[1].wait()
+    kv_copies(1)[1].start()
+    for d in wo_order:
+        wo_copy(d).start()
     q_high = dot(normed, wq[:, 512:1024])
     kn[...] = rotate(rms_scale(keys, kgain[...])).astype(BF).astype(F32)
     for h in range(8):
@@ -193,17 +194,13 @@
 
     for i in range(2):
         q = qs[i * 16 : (i + 1) * 16].reshape(128, 128)
-        q_t = q.T
         own = jnp.sum((q * spread(kn, i)).T, axis=0, keepdims=True) * scale
-        weights = jnp.concatenate(
-            [jnp.where(lane_request == j, q_t, 0.0).astype(BF) for j in range(16)], axis=0
-        )
         length = jnp.zeros((1, 128), jnp.int32)
         for j in range(16):
             length = jnp.where(lane_request[0:1] == j, lens[i * 16 + j], length)
         kv_copies(i)[0].wait()
-        keys_all = jnp.concatenate([kc[i * 16 + j] for j in range(16)], axis=1)
-        s = dot(keys_all, weights) * scale
+        s = [dot_t(q[j * 8 : (j + 1) * 8].astype(BF), kc[i * 16 + j]) for j in range(16)]
+        s = jnp.concatenate(s, axis=0).T * scale
         s = jnp.where(where_p < length, s, -jnp.inf)
         top = jnp.maximum(jnp.max(s, axis=0, keepdims=True), own)
         ex = jnp.exp(s - top)
@@ -441,15 +438,9 @@
     def scatter(q, src, dst, sem, to):
         return remote(src, dst, s_send.at[q], s_recv.at[q, sem], to)
 
-    def first(q, order, what, way):
-        side = 0 if way > 0 else 1
+    def first(q, order, way):
         to = moved(co, order[2], way)
-        if what == "far":
-            src = block(ya, q, order[:2], moved(co, order[2], 2), side)
-            return scatter(q, src, r1u.at[q, side], side, to)
-        half = 1 - side if what == "near" else side
-        src = block(ya, q, order[:2], to, half)
-        return scatter(q, src, r1.at[q, side, 2 * half : 2 * half + 2], 2, to)
+        return scatter(q, block(ya, q, order[:2], to), r1.at[q, way - 1], 0, to)
 
     def left_axes(order):
         return [a for a in ("y", "z", "x") if a != order[2]]
@@ -460,27 +451,18 @@
         return scatter(q, s1.at[q, to[a], to[b]], r2.at[q, i * 4 + j - 1], 3, to)
 
     def scatter1(q, order):
-        first(q, order, "far", 1).start()
-        first(q, order, "far", -1).start()
-        first(q, order, "near", 1).start()
-        first(q, order, "near", -1).start()
+        for way in (2, 1, 3):
+            first(q, order, way).start()
 
     def pair_add(q):
         pair_copy(q).wait_recv()
         own = ya.at[q, me_c]
         own[...] = (own[...].astype(F32) + ysib[q].astype(F32)).astype(BF)
 
-    def scatter_relay(q, order):
-        for way, side in ((1, 0), (-1, 1)):
-            first(q, order, "far", way).wait_recv()
-            mine = block(ya, q, order[:2], moved(co, order[2], way), side)
-            mine[...] = (mine[...].astype(F32) + r1u[q, side].astype(F32)).astype(BF)
-            first(q, order, "relayed", way).start()
-
     def scatter2(q, order):
-        pltpu.make_async_copy(r1.at[q], r1.at[q], s_recv.at[q, 2]).wait()
+        pltpu.make_async_copy(r1.at[q], r1.at[q], s_recv.at[q, 0]).wait()
         own = block(ya, q, order[:2], co)[...].astype(F32)
-        s1[q] = (own + r1[q, 0].astype(F32) + r1[q, 1].astype(F32)).astype(BF)
+        s1[q] = (own + r1[q, 0].astype(F32) + r1[q, 1].astype(F32) + r1[q, 2].astype(F32)).astype(BF)
         for j in (2, 1, 3, 0):
             for i in (2, 1, 3, 0):
                 if i or j:
@@ -505,7 +487,6 @@
     token_sums(2)
     pair_add(1)
     scatter1(1, ORDER_B)
-    last_part(scatter_relay)
     pair_add(2)
     scatter1(2, ORDER_C)
 
@@ -515,9 +496,6 @@
         fn(1, ORDER_B)
         fn(2, ORDER_C)
 
-    scatter_relay(0, ORDER_A)
-    scatter_relay(1, ORDER_B)
-    scatter_relay(2, ORDER_C)
     order_of_end(scatter2)
     order_of_end(finish)
 
@@ -552,7 +530,7 @@
             vmem((4, 2, 4, 4, 4, 32, 128), BF), vmem((4, 128, 256), BF), vmem((4, 256, 128), BF),
             vmem((4, 128, 128), F32), vmem((4, 128, 384), F32), vmem((4, 128, 128), F32),
             vmem((4, 2, 4, 4, 4, 32, 128), BF), vmem((4, 4, 4, 4, 32, 128), BF),
-            vmem((4, 2, 2, 4, 32, 128), BF), vmem((4, 2, 4, 4, 32, 128), BF), vmem((4, 4, 4, 32, 128), BF),
+            vmem((4, 2, 2, 4, 32, 128), BF), vmem((4, 3, 4, 4, 32, 128), BF), vmem((4, 4, 4, 32, 128), BF),
             vmem((4, 15, 32, 128), BF),
             vmem((32, 512), F32), vmem((127, 32, 128), BF),
             dma((11,)), dma((2, 2)), dma((4,)), dma((4,)),

time: 62.3 us -> 57.6 us (0.925)
  Pallas kernels: 60.2 us -> 56.1 us
    pallas_call x1, Pallas kernels: 60.2 us -> 56.1 us  [per_device(): pl.pallas_call(layer_kernel, out_shape=jax.ShapeDtypeStruct((32, 512), BF...]
where the time goes in v4:
time: 57.6 us; the launch traced here: 57.5 us
  Pallas kernels  56.1 us (97%)
  local copies, waits for them, and re-layouts  1.38 us (2%)
    pallas_call x1, Pallas kernels, per_device(): pl.pallas_call(layer_kernel, out_shape=jax.ShapeDtypeStruct((32, 512), BF...  56.1 us
    unnamed x1, local copies, waits for them, and re-layouts  1.38 us

profile of v4, /device:TPU:0, one launch (start us, length us, event | category | flops | bytes accessed | tf_op | source)
XLA Modules:
  0.0 57.5 jit_solution(11224668368966820673)
XLA Ops:
  0.0 56.1 %layer.1 = bf16[32,512]{1,0:T(8,128)(2,1)} custom-call(bf16[32,2048]{1,0:T(8,128)(2,1)} %hidden_h.1, f32[1,2048]{1,0:T(1,128)} %bitcast.13, f32[1,2048]{1,0:T(1,128)} %bitcast.14, bf16[2048,1024]{1,0:T(8,128)(2,1)} %wq_h.1, bf16[2048,128]{1,0:T(8,128)(2,1)} %wk_h.1, bf16[2048,128]{1,0:T(8,128)(2,1)} %wv_h.1, f32[1,128]{1,0:T(1,128)} %bitcast.16, ...), custom_call_target="tpu_custom_call" | custom-call | tf_op jit(solution)/shard_map/layer/pallas_call | solution.py:517
  56.1 1.4 %copy.19 = bf16[32,512]{1,0:T(8,128)(2,1)} copy(bf16[32,512]{1,0:T(8,128)(2,1)} %layer.1) | data formatting | bytes 65536

commit v5 on v4

--- a/solution.py
+++ b/solution.py
@@ -170,7 +170,6 @@
     lane8 = lax.broadcasted_iota(jnp.int32, (8, 128), 1)
     idv = ids[...]
     ids_all[grp] = jnp.where(lane8 // 32 == co["x"], jnp.concatenate([idv] * 4, axis=1), -1)
-    pl.semaphore_wait(bar, 34)
 
     def ids_copy(d):
         return pltpu.make_async_remote_copy(
@@ -182,7 +181,6 @@
         ids_copy(d).start()
         return 0
 
-    lax.fori_loop(1, 32, ids_start, 0)
 
     scale = 128 ** -0.5
     lane_request = lax.broadcasted_iota(jnp.int32, (128, 128), 1) // 8
@@ -221,10 +219,12 @@
     def t_copy(d):
         return remote(terms.at[d - 1], tin.at[d - 1], t_send, t_recv.at[d - 1], moved(co, "y", d))
 
+    pl.semaphore_wait(bar, 34)
     for d in wo_order[:3]:
         wo_copy(d).wait()
         terms[d - 1] = dot(heads, wo[d]).astype(BF)
         t_copy(d).start()
+    lax.fori_loop(1, 32, ids_start, 0)
     wo_copy(0).wait()
     mid = hidden[:, quarter(me_y)].astype(F32) + dot(heads, wo[0]).astype(BF).astype(F32)
     for d in (1, 3, 2):

time: 57.6 us -> 57.6 us (level)
  no operation moved by 1% of the time
where the time goes in v5:
time: 57.6 us; the launch traced here: 57.3 us
  Pallas kernels  55.9 us (97%)
  local copies, waits for them, and re-layouts  1.38 us (2%)
    pallas_call x1, Pallas kernels, per_device(): pl.pallas_call(layer_kernel, out_shape=jax.ShapeDtypeStruct((32, 512), BF...  55.9 us
    unnamed x1, local copies, waits for them, and re-layouts  1.38 us

profile of v5, /device:TPU:0, one launch (start us, length us, event | category | flops | bytes accessed | tf_op | source)
XLA Modules:
  0.0 57.3 jit_solution(11740707260130086802)
XLA Ops:
  0.0 55.9 %layer.1 = bf16[32,512]{1,0:T(8,128)(2,1)} custom-call(bf16[32,2048]{1,0:T(8,128)(2,1)} %hidden_h.1, f32[1,2048]{1,0:T(1,128)} %bitcast.13, f32[1,2048]{1,0:T(1,128)} %bitcast.14, bf16[2048,1024]{1,0:T(8,128)(2,1)} %wq_h.1, bf16[2048,128]{1,0:T(8,128)(2,1)} %wk_h.1, bf16[2048,128]{1,0:T(8,128)(2,1)} %wv_h.1, f32[1,128]{1,0:T(1,128)} %bitcast.16, ...), custom_call_target="tpu_custom_call" | custom-call | tf_op jit(solution)/shard_map/layer/pallas_call | solution.py:517
  55.9 1.4 %copy.19 = bf16[32,512]{1,0:T(8,128)(2,1)} copy(bf16[32,512]{1,0:T(8,128)(2,1)} %layer.1) | data formatting | bytes 65536
